TPU v7x, 256 devices: a whole 4x4x8 slice. The times are simulated.
256 devices in a mesh: rows: 64 (over z_lo, y, x), cols: 4 (over z_hi, core).
Axes of the slice: x: 4, y: 4, z: 8 (z_hi: 2, z_lo: 4; z = z_hi * 4 + z_lo), core: 2. Of those that a mesh axis runs over, the one named last changes fastest.
Arguments:
- elevation: float32 [4096, 4096], P(('rows', 'cols')), may hold values from -2.4 to 2.4
- potential: float32 [4096, 4096], P(('rows', 'cols')), may hold values from -6 to 6
- elevation_cot: float32 [4096, 4096], P(('rows', 'cols')), may hold values from -6 to 6
- potential_cot: float32 [4096, 4096], P(('rows', 'cols')), may hold values from -6 to 6
Outputs:
- elevation_grad: float32 [4096, 4096], P(('rows', 'cols'))
- potential_grad: float32 [4096, 4096], P(('rows', 'cols'))
All inputs are finite; a program needn't handle non-finite values.
Results may differ from a plain program's by a relative error of at most 0.00011.
Values sent between devices are 32-bit elements; how exact they have to be, the bound alone decides.
No kernel may reach another device: no remote copies, remote signals or barrier semaphores. Data moves between devices by JAX's collectives and lax.ppermute only.
A program may use at most 128 MiB of HBM per device.

v0:
```python
import functools

import jax
import jax.numpy as jnp
import numpy as np
from jax import lax
from jax.experimental import pallas as pl
from jax.experimental.pallas import tpu as pltpu
from jax.sharding import PartitionSpec as P

stiffness = 0.05
section_step = 0.25
side = 4096
devices = 256
local_rows = 16
radix = 16
fine = 256
kept_y = 64
kept_a = np.array([0, 1, 2, 3, 12, 13, 14, 15])
mesh_axes = ("rows", "cols")


def split_table(table):
    table = table.astype(np.float32)
    high = table.astype(jnp.bfloat16)
    low = (table - high.astype(np.float32)).astype(jnp.bfloat16)
    return np.stack((high, low), 0)


@functools.lru_cache(maxsize=None)
def tables():
    two_pi = 2.0 * np.pi
    eye_j = np.eye(local_rows)
    residue = np.arange(radix)
    angle = two_pi * np.outer(np.arange(radix), residue) / radix
    parts = np.stack((np.cos(angle), -np.sin(angle)), 0).reshape(2, radix, 4, 4)
    right_y = np.einsum("cthl,jk->tjhckl", parts, eye_j).reshape(radix * local_rows, 512)
    angle = two_pi * np.outer(np.arange(fine), residue) / side
    cosine = np.cos(angle).reshape(fine, 4, 1, 1, 4)
    sine = np.sin(angle).reshape(fine, 4, 1, 1, 4)
    signs = np.array([1.0, -1.0]).reshape(1, 1, 2, 1, 1)
    full = (fine, 4, 2, local_rows, 4)
    twist_y = np.stack(
        (np.broadcast_to(cosine, full).reshape(fine, 512), np.broadcast_to(sine * signs, full).reshape(fine, 512)), 0
    )
    angle = two_pi * np.outer(np.arange(kept_y), np.arange(fine)) / fine
    left_y = np.concatenate((np.cos(angle), np.sin(angle)), 0)
    left_y_back = left_y.T
    angle = two_pi * np.outer(np.arange(fine), np.arange(fine)) / fine
    left_x = np.concatenate((np.cos(angle), np.sin(angle)), 0)
    angle = two_pi * np.outer(np.arange(fine), np.arange(local_rows)) / side
    full = (fine, 2, local_rows, 4)
    signs = np.array([1.0, -1.0]).reshape(1, 2, 1, 1)
    twist_x = np.stack(
        (
            np.broadcast_to(np.cos(angle)[:, None, :, None], full).reshape(fine, 128),
            np.broadcast_to(np.sin(angle)[:, None, :, None] * signs, full).reshape(fine, 128),
        ),
        0,
    )
    angle = two_pi * np.outer(np.arange(local_rows), kept_a) / radix
    cosine, sine = (np.cos(angle), np.sin(angle))
    eye_q = np.eye(4)
    forward = np.array([[cosine, -sine], [sine, cosine]])
    right_x = np.einsum("cdja,qp->cjqdap", forward, eye_q).reshape(128, 64)
    turned = np.array([[-sine, cosine], [-cosine, -sine]])
    right_x_back = right_x.T
    right_x_turn = np.einsum("cdja,qp->caqdjp", turned, eye_q).reshape(64, 128)
    return dict(
        right_y=split_table(right_y),
        right_y_back=split_table(right_y.T),
        left_y=split_table(left_y),
        left_y_back=split_table(left_y_back),
        twist_y=twist_y.astype(np.float32),
        left_x=split_table(left_x),
        right_x=split_table(right_x),
        right_x_back=split_table(right_x_back),
        right_x_turn=split_table(right_x_turn),
        twist_x=twist_x.astype(np.float32),
    )


y_in = ("right_y", "twist_y", "left_y")
y_out = ("left_y_back", "twist_y", "right_y_back")
y_both = ("left_y_back", "twist_y", "right_y_back", "right_y", "left_y")
x_in = ("left_x", "twist_x", "right_x")
x_out = ("right_x_back", "right_x_turn", "twist_x", "left_x")
x_both = ("left_x", "twist_x", "right_x", "right_x_back")
x_turn = ("left_x", "twist_x", "right_x", "right_x_turn")
x_all = ("left_x", "twist_x", "right_x", "right_x_back", "right_x_turn")


def parted(values):
    high = values.astype(jnp.bfloat16)
    return (high, (values - high.astype(jnp.float32)).astype(jnp.bfloat16))


def product(first, second):
    return jnp.dot(first, second, preferred_element_type=jnp.float32)


def left_times(table_ref, values):
    high, low = parted(values)
    return product(table_ref[0], high) + (product(table_ref[1], high) + product(table_ref[0], low))


def times_right(values, table_ref):
    high, low = parted(values)
    return product(high, table_ref[0]) + (product(low, table_ref[0]) + product(high, table_ref[1]))


def swapped(values):
    pieces = [
        pltpu.roll(values[:, start : start + 128], 64, 1) for start in range(0, values.shape[1], 128)
    ]
    return pieces[0] if len(pieces) == 1 else jnp.concatenate(pieces, 1)


def half_signs(shape):
    lane = lax.broadcasted_iota(jnp.int32, shape, 1)
    return jnp.where(lane % 128 < 64, 1.0, -1.0).astype(jnp.float32)


def y_forward(tab, field, message_ref, slot, count):
    values = times_right(field, tab["right_y"])
    values = values * tab["twist_y"][0] + swapped(values) * tab["twist_y"][1]
    both = left_times(tab["left_y"], values)
    turned = swapped(both[kept_y:])
    values = both[:kept_y] + turned * half_signs(turned.shape)
    for part in range(4):
        message_ref[pl.ds(part * count + slot, kept_y, stride=4 * count), :] = values[
            :, part * 128 : part * 128 + 128
        ]


def y_inverse(tab, arrived_ref, slot, count):
    values = jnp.concatenate(
        [arrived_ref[pl.ds(part * count + slot, kept_y, stride=4 * count), :] for part in range(4)], 1
    )
    turned = swapped(values)
    stacked = jnp.concatenate((values, turned * -half_signs(turned.shape)), 0)
    values = left_times(tab["left_y_back"], stacked)
    values = values * tab["twist_y"][0] - swapped(values) * tab["twist_y"][1]
    return times_right(values, tab["right_y_back"])


def x_forward(tab, arrived_ref, slot, count):
    values = arrived_ref[pl.ds(slot, fine, stride=count), :] if count > 1 else arrived_ref[...]
    both = left_times(tab["left_x"], values)
    turned = swapped(both[fine:])
    values = both[:fine] + turned * half_signs(turned.shape)
    values = values * tab["twist_x"][0] + swapped(values) * tab["twist_x"][1]
    return times_right(values, tab["right_x"])


def x_inverse(tab, straight, turned_part, message_ref, slot, count):
    if straight is None:
        values = times_right(turned_part, tab["right_x_turn"])
    else:
        values = times_right(straight, tab["right_x_back"])
        if turned_part is not None:
            values = values + times_right(turned_part, tab["right_x_turn"])
    values = values * tab["twist_x"][0] - swapped(values) * tab["twist_x"][1]
    both = left_times(tab["left_x"], values)
    turned = swapped(both[fine:])
    values = both[:fine] - turned * half_signs(turned.shape)
    put(message_ref, values, slot, count)


def put(message_ref, values, slot, count):
    if count > 1:
        message_ref[pl.ds(slot, fine, stride=count), :] = values
    else:
        message_ref[...] = values


def message(count):
    return jax.ShapeDtypeStruct((devices * count, 128), jnp.float32)


field_shape = jax.ShapeDtypeStruct((256, 256), jnp.float32)
spectrum_shape = jax.ShapeDtypeStruct((fine, 64), jnp.float32)


class Fetched:
    def __init__(self, source, target, semaphore):
        self.target = target
        self.copy = pltpu.make_async_copy(source, target, semaphore)
        self.copy.start()
        self.pending = True

    def arrive(self):
        if self.pending:
            self.copy.wait()
            self.pending = False

    def __getitem__(self, index):
        self.arrive()
        return self.target[index]


def run(body, names, inputs, outputs, flops):
    operands = [inputs[0]] + [jnp.asarray(tables()[name]) for name in names] + list(inputs[1:])
    total_in = len(operands)
    total = total_in + len(outputs)

    def kernel(*refs):
        semaphores = refs[-1]
        held = refs[total:-1]
        fetched = [Fetched(refs[i], held[i], semaphores.at[i]) for i in range(total_in)]
        tab = dict(zip(names, fetched[1 : 1 + len(names)]))
        ins = fetched[:1] + fetched[1 + len(names) :]
        outs = held[total_in:]
        sends = {}

        def emit(place):
            copy = pltpu.make_async_copy(
                outs[place], refs[total_in + place], semaphores.at[total_in + place]
            )
            copy.start()
            sends[place] = copy

        body(tab, ins, outs, emit)
        for place in range(len(outs)):
            if place not in sends:
                emit(place)
        for item in fetched:
            item.arrive()
        for copy in sends.values():
            copy.wait()

    outside = pl.BlockSpec(memory_space=pltpu.HBM)
    moved = sum(4 * int(np.prod(a.shape)) for a in list(operands) + list(outputs))
    return pl.pallas_call(
        kernel,
        out_shape=list(outputs),
        in_specs=[outside] * total_in,
        out_specs=[outside] * len(outputs),
        scratch_shapes=[pltpu.VMEM(a.shape, a.dtype) for a in list(operands) + list(outputs)]
        + [pltpu.SemaphoreType.DMA((total,))],
        compiler_params=pltpu.CompilerParams(vmem_limit_bytes=60_000_000),
        cost_estimate=pl.CostEstimate(flops=int(flops * 6e8), bytes_accessed=int(moved), transcendentals=0),
    )(*operands)


def exchange(values):
    count = values.shape[0] // devices
    values = values.reshape(devices, count, 128)
    values = lax.all_to_all(values, mesh_axes, split_axis=0, concat_axis=0, tiled=True)
    return values.reshape(devices * count, 128)


def gather_rows(block):
    pieces = [block[:, start : start + 256] for start in range(0, side, 256)]
    return jnp.concatenate(pieces, 0).T


def scatter_rows(out_ref, field, extra_ref):
    turned = field.T
    for part in range(radix):
        columns = pl.ds(part * 256, 256)
        out_ref[:, columns] = turned[part * local_rows : (part + 1) * local_rows, :] + extra_ref[:, columns]


def wave_tables():
    own = lax.axis_index("rows") * lax.axis_size("cols") + lax.axis_index("cols")
    lane = jnp.arange(64, dtype=jnp.int32)
    digit = (lane // 4) % 8
    mode_y = 4 * own + lane % 4
    row = jnp.arange(fine, dtype=jnp.int32)
    mode_x = 256 * jnp.where(digit < 4, digit, digit - 8)[None, :] + row[:, None]
    wave_x = (2.0 * jnp.pi / side) * mode_x.astype(jnp.float32)
    wave_y = jnp.broadcast_to(((2.0 * jnp.pi / side) * mode_y.astype(jnp.float32))[None, :], wave_x.shape)
    weight = jnp.where(mode_y == 0, 1.0, 2.0)[None, :] / (side * side)
    keep = jnp.where(jnp.abs(mode_x) < side // 4, weight, 0.0).astype(jnp.float32)
    magnitude = jnp.sqrt(wave_x * wave_x + wave_y * wave_y)
    return jnp.stack((keep, magnitude, wave_x, wave_y), 0)


def per_device(elevation, potential, elevation_cot, potential_cot):
    waves = wave_tables()

    def start(tab, ins, outs, emit):
        surface = gather_rows(ins[0][...])
        outs[0][...] = surface
        emit(0)
        y_forward(tab, gather_rows(ins[1][...]), outs[1], 1, 2)
        y_forward(tab, surface, outs[1], 0, 2)

    elev, sent = run(start, y_in, (elevation, potential), (field_shape, message(2)), 2)
    first = exchange(sent)

    def cotangents(tab, ins, outs, emit):
        outs[0][...] = section_step * gather_rows(ins[0][...])
        rate = section_step * gather_rows(ins[1][...])
        outs[1][...] = rate
        y_forward(tab, -stiffness * rate, outs[2], 0, 1)

    rate_elev, rate_pot, bend_sent = run(
        cotangents, y_in, (elevation_cot, potential_cot), (field_shape, field_shape, message(1)), 1
    )

    def second(tab, ins, outs, emit):
        spec = x_forward(tab, ins[0], 1, 2)
        outs[1][...] = spec * ins[1][0]
        spec = spec * ins[1][0]
        for degree in range(4):
            spec = spec * ins[1][1]
            x_inverse(tab, spec, None, outs[0], degree, 4)

    sent, pot_spec = run(second, x_both, (first, waves), (message(4), spectrum_shape), 2)
    lifts = exchange(sent)

    def slopes(tab, ins, outs, emit):
        spec = x_forward(tab, ins[0], 0, 2) * ins[2][0]
        x_inverse(tab, None, spec * ins[2][2], outs[0], 0, 1)
        x_inverse(tab, None, spec * ins[2][3], outs[1], 0, 1)
        spec = ins[1][...]
        x_inverse(tab, None, spec * ins[2][2], outs[2], 0, 1)
        x_inverse(tab, None, spec * ins[2][3], outs[3], 0, 1)

    slope_x_sent, slope_y_sent, flow_x_sent, flow_y_sent = run(
        slopes, x_turn, (first, pot_spec, waves), (message(1),) * 4, 2
    )

    def third(tab, ins, outs, emit):
        lifted = y_inverse(tab, ins[0], 0, 4)
        outs[1][...] = lifted
        emit(1)
        y_forward(tab, -ins[1][...] * lifted, outs[0], 0, 2)
        put(outs[0], ins[2][...], 1, 2)

    sent, lift_11 = run(third, y_both, (lifts, elev, bend_sent), (message(2), field_shape), 2)
    arrived = exchange(sent)

    def inverse_of(slots, count):
        def body(tab, ins, outs, emit):
            for place, slot in enumerate(slots):
                outs[place][...] = y_inverse(tab, ins[0], slot, count)
                emit(place)

        return body

    lift_12, lift_13, lift_14 = run(inverse_of((1, 2, 3), 4), y_out, (lifts,), (field_shape,) * 3, 3)

    def fourth(tab, ins, outs, emit):
        spec = x_forward(tab, ins[0], 0, 2) * ins[1][0]
        for degree in range(3):
            spec = spec * ins[1][1]
            x_inverse(tab, spec, None, outs[0], degree, 4)
        put(outs[0], ins[2][...], 3, 4)

    (sent,) = run(fourth, x_both, (arrived, waves, slope_x_sent), (message(4),), 2)

    def spectra_of(slots, count):
        def body(tab, ins, outs, emit):
            for place, slot in enumerate(slots):
                outs[place][...] = x_forward(tab, ins[0], slot, count) * ins[1][0]

        return body

    (bend_spec,) = run(spectra_of((1,), 2), x_in, (arrived, waves), (spectrum_shape,), 1)
    arrived = exchange(sent)

    def fifth(tab, ins, outs, emit):
        lifted = y_inverse(tab, ins[0], 0, 4)
        outs[1][...] = lifted
        emit(1)
        surface = ins[1][...]
        y_forward(tab, -surface * lifted - (surface * surface / 2.0) * ins[2][...], outs[0], 0, 1)

    sent, lift_21 = run(fifth, y_both, (arrived, elev, lift_12), (message(1), field_shape), 2)
    lift_22, lift_23, slope_x = run(inverse_of((1, 2, 3), 4), y_out, (arrived,), (field_shape,) * 3, 3)
    arrived = exchange(sent)

    def sixth(tab, ins, outs, emit):
        spec = x_forward(tab, ins[0], 0, 1) * ins[1][0]
        for degree in range(2):
            spec = spec * ins[1][1]
            x_inverse(tab, spec, None, outs[0], degree, 4)
        put(outs[0], ins[2][...], 2, 4)
        put(outs[0], ins[3][...], 3, 4)

    (sent,) = run(sixth, x_both, (arrived, waves, slope_y_sent, flow_x_sent), (message(4),), 2)
    arrived = exchange(sent)

    def seventh(tab, ins, outs, emit):
        lifted = y_inverse(tab, ins[0], 0, 4)
        outs[1][...] = lifted
        emit(1)
        surface = ins[1][...]
        square = surface * surface / 2.0
        cube = square * surface / 3.0
        y_forward(tab, -surface * lifted - square * ins[2][...] - cube * ins[3][...], outs[0], 0, 1)

    sent, lift_31 = run(seventh, y_both, (arrived, elev, lift_22, lift_13), (message(1), field_shape), 2)
    lift_32, slope_y, flow_x = run(inverse_of((1, 2, 3), 4), y_out, (arrived,), (field_shape,) * 3, 3)
    arrived = exchange(sent)

    def eighth(tab, ins, outs, emit):
        spec = x_forward(tab, ins[0], 0, 1) * (ins[1][0] * ins[1][1])
        x_inverse(tab, spec, None, outs[0], 0, 2)
        put(outs[0], ins[2][...], 1, 2)

    (sent,) = run(eighth, x_both, (arrived, waves, flow_y_sent), (message(2),), 1)
    arrived = exchange(sent)

    square = elev * elev / 2.0
    cube = square * elev / 3.0
    partial = (
        lift_11
        + lift_21
        + lift_31
        + elev * (lift_12 + lift_22 + lift_32)
        + square * (lift_13 + lift_23)
        + cube * lift_14
    )
    growth = lift_12 + lift_22 + lift_32 + elev * (lift_13 + lift_23) + square * lift_14
    steepness = 1.0 + slope_x * slope_x + slope_y * slope_y

    def ninth(tab, ins, outs, emit):
        vertical = ins[1][...] + y_inverse(tab, ins[0], 0, 2)
        vertical_cot = ins[2][...] * (ins[3][...] + vertical * ins[4][...])
        outs[1][...] = vertical
        emit(1)
        outs[2][...] = vertical_cot
        emit(2)
        y_forward(tab, vertical_cot, outs[0], 0, 2)
        y_forward(tab, ins[5][...] * vertical_cot, outs[0], 1, 2)

    sent, vertical, vertical_cot = run(
        ninth,
        y_both,
        (arrived, partial, steepness, rate_elev, rate_pot, elev),
        (message(2), field_shape, field_shape),
        3,
    )
    (flow_y,) = run(inverse_of((1,), 2), y_out, (arrived,), (field_shape,), 1)
    arrived = exchange(sent)
    steep_cot = vertical * rate_elev + 0.5 * vertical * vertical * rate_pot

    def forward_all(tab, ins, outs, emit):
        for place in range(len(ins)):
            y_forward(tab, ins[place][...], outs[place], 0, 1)
            emit(place)

    def sends_of(*fields):
        return run(forward_all, y_in, fields, (message(1),) * len(fields), len(fields))

    square_cot_sent, cube_cot_sent = sends_of(square * vertical_cot, cube * vertical_cot)
    slope_x_cot, slope_y_cot = sends_of(
        -flow_x * rate_elev + 2.0 * slope_x * steep_cot, -flow_y * rate_elev + 2.0 * slope_y * steep_cot
    )
    flow_x_cot, flow_y_cot = sends_of(
        -slope_x * rate_elev - flow_x * rate_pot, -slope_y * rate_elev - flow_y * rate_pot
    )

    def tenth(tab, ins, outs, emit):
        spec = x_forward(tab, ins[0], 0, 2) * ins[1][0]
        outs[1][...] = spec
        emit(1)
        x_inverse(tab, spec * ins[1][1], None, outs[0], 0, 1)

    sent, cot_spec = run(tenth, x_both, (arrived, waves), (message(1), spectrum_shape), 1)
    (elev_cot_spec,) = run(spectra_of((1,), 2), x_in, (arrived, waves), (spectrum_shape,), 1)
    arrived = exchange(sent)

    def eleventh(tab, ins, outs, emit):
        lifted = y_inverse(tab, ins[0], 0, 1)
        outs[1][...] = lifted
        emit(1)
        surface = ins[1][...]
        y_forward(tab, surface * lifted, outs[0], 0, 4)
        y_forward(tab, (surface * surface / 2.0) * lifted, outs[0], 1, 4)
        put(outs[0], ins[2][...], 2, 4)
        put(outs[0], ins[3][...], 3, 4)

    sent, fourth_cot = run(
        eleventh, y_both, (arrived, elev, square_cot_sent, cube_cot_sent), (message(4), field_shape), 3
    )
    (cube_fourth_sent,) = sends_of(cube * fourth_cot)
    arrived = exchange(sent)

    def twelfth(tab, ins, outs, emit):
        spec = x_forward(tab, ins[0], 0, 4) * ins[1][0]
        spec = ins[1][1] * ((ins[2][...] - spec) + ins[1][1] * ins[3][...])
        x_inverse(tab, spec, None, outs[0], 0, 1)

    (sent,) = run(twelfth, x_both, (arrived, waves, cot_spec, elev_cot_spec), (message(1),), 1)
    square_fourth_spec, square_cot_spec, cube_cot_spec = run(
        spectra_of((1, 2, 3), 4), x_in, (arrived, waves), (spectrum_shape,) * 3, 1
    )
    arrived = exchange(sent)

    def thirteenth(tab, ins, outs, emit):
        lifted = y_inverse(tab, ins[0], 0, 1)
        outs[1][...] = lifted
        emit(1)
        y_forward(tab, ins[1][...] * lifted, outs[0], 0, 4)
        for slot in range(1, 4):
            put(outs[0], ins[1 + slot][...], slot, 4)

    sent, third_cot = run(
        thirteenth,
        y_both,
        (arrived, elev, cube_fourth_sent, slope_x_cot, slope_y_cot),
        (message(4), field_shape),
        2,
    )
    (square_third_sent,) = sends_of(square * third_cot)
    arrived = exchange(sent)

    def fourteenth(tab, ins, outs, emit):
        wave = ins[1][1]
        spec = x_forward(tab, ins[0], 0, 4) * ins[1][0]
        spec = wave * (
            (ins[2][...] - spec) + wave * ((ins[3][...] - ins[4][...]) + wave * ins[5][...])
        )
        x_inverse(tab, spec, None, outs[0], 0, 1)

    (sent,) = run(
        fourteenth,
        x_both,
        (arrived, waves, cot_spec, elev_cot_spec, square_fourth_spec, square_cot_spec),
        (message(1),),
        1,
    )

    def gathered(tab, ins, outs, emit):
        wave = ins[1][1]
        cube_fourth = x_forward(tab, ins[0], 1, 4) * ins[1][0]
        outs[0][...] = wave * (
            ins[2][...]
            + wave * (ins[3][...] + wave * ((ins[4][...] - cube_fourth) + wave * ins[5][...]))
        )
        slope_x_spec = x_forward(tab, ins[0], 2, 4) * ins[1][0]
        slope_y_spec = x_forward(tab, ins[0], 3, 4) * ins[1][0]
        outs[1][...] = -(ins[1][2] * slope_x_spec + ins[1][3] * slope_y_spec)
        outs[2][...] = ins[6][...] * (wave * wave) * (wave * wave)

    pot_part, elev_turn, elev_part = run(
        gathered,
        x_in,
        (arrived, waves, cot_spec, elev_cot_spec, square_cot_spec, cube_cot_spec, bend_spec),
        (spectrum_shape,) * 3,
        1,
    )
    arrived = exchange(sent)

    def fifteenth(tab, ins, outs, emit):
        lifted = y_inverse(tab, ins[0], 0, 1)
        outs[1][...] = lifted
        emit(1)
        y_forward(tab, ins[1][...] * lifted, outs[0], 0, 4)
        for slot in range(1, 4):
            put(outs[0], ins[1 + slot][...], slot, 4)

    sent, second_cot = run(
        fifteenth,
        y_both,
        (arrived, elev, square_third_sent, flow_x_cot, flow_y_cot),
        (message(4), field_shape),
        2,
    )
    arrived = exchange(sent)

    def elevation_side(tab, ins, outs, emit):
        x_inverse(tab, ins[0][...], ins[1][...], outs[0], 0, 1)

    (elev_sent,) = run(elevation_side, x_out, (elev_part, elev_turn), (message(1),), 1)

    def sixteenth(tab, ins, outs, emit):
        wave = ins[1][1]
        keep = ins[1][0]
        first_part = x_forward(tab, ins[0], 0, 4) * keep
        second_part = x_forward(tab, ins[0], 1, 4) * keep
        flow_part = x_forward(tab, ins[0], 2, 4) * ins[1][2] + x_forward(tab, ins[0], 3, 4) * ins[1][3]
        straight = ins[2][...] - wave * (first_part + wave * second_part)
        x_inverse(tab, straight, -flow_part * keep, outs[0], 1, 2)
        put(outs[0], ins[3][...], 0, 2)

    (sent,) = run(sixteenth, x_all, (arrived, waves, pot_part, elev_sent), (message(2),), 2)
    arrived = exchange(sent)

    grad = (
        vertical_cot * growth
        - (lift_31 + elev * lift_22 + square * lift_13) * fourth_cot
        - (lift_21 + elev * lift_12) * third_cot
        - lift_11 * second_cot
        - rate_pot
    )

    def finish(tab, ins, outs, emit):
        scatter_rows(outs[1], y_inverse(tab, ins[0], 1, 2), ins[3])
        emit(1)
        scatter_rows(outs[0], ins[1][...] + y_inverse(tab, ins[0], 0, 2), ins[2])

    block = jax.ShapeDtypeStruct(elevation.shape, jnp.float32)
    elevation_grad, potential_grad = run(
        finish, y_out, (arrived, grad, elevation_cot, potential_cot), (block, block), 2
    )
    return (elevation_grad, potential_grad)


def solution(mesh):
    spec = P(mesh_axes, None)
    return jax.shard_map(
        per_device, mesh=mesh, in_specs=(spec,) * 4, out_specs=(spec, spec), check_vma=False
    )
```

profile of v0, /device:TPU:1, one launch (start us, length us, event | category | flops | bytes accessed | tf_op | source)
XLA Modules:
  0.0 465.1 jit_solution(11950690810064190531)
XLA Ops:
  0.6 4.0 shard_map.149
  4.6 15.7 %all-to-all-start = ((f32[256,2,128]{2,1,0:T(2,128)}), f32[256,2,128]{2,1,0:T(2,128)S(1)}, u32[]{:S(2)}, u32[]{:S(2)}) async-start(f32[256,2,128]{2,1,0:T(2,128)} %bitcast.69), calls=%async_computation | async-start | bytes 524288 | tf_op jit(solution)/shard_map/all_to_all | solution.py:249
  21.3 14.8 %all-to-all-done = f32[256,2,128]{2,1,0:T(2,128)S(1)} async-done(((f32[256,2,128]{2,1,0:T(2,128)}), f32[256,2,128]{2,1,0:T(2,128)S(1)}, u32[]{:S(2)}, u32[]{:S(2)}) %all-to-all-start) | async-done | bytes 262176 | tf_op jit(solution)/shard_map/all_to_all | solution.py:249
  36.8 4.6 shard_map.150
  41.4 5.7 %all-to-all-start.1 = ((f32[256,4,128]{2,1,0:T(4,128)}), f32[256,4,128]{2,1,0:T(4,128)S(1)}, u32[]{:S(2)}, u32[]{:S(2)}) async-start(f32[256,4,128]{2,1,0:T(4,128)} %bitcast.61), calls=%async_computation.1 | async-start | bytes 1048576 | tf_op jit(solution)/shard_map/all_to_all | solution.py:249
  47.1 3.4 shard_map.151
  50.5 18.1 %all-to-all-done.1 = f32[256,4,128]{2,1,0:T(4,128)S(1)} async-done(((f32[256,4,128]{2,1,0:T(4,128)}), f32[256,4,128]{2,1,0:T(4,128)S(1)}, u32[]{:S(2)}, u32[]{:S(2)}) %all-to-all-start.1) | async-done | bytes 524320 | tf_op jit(solution)/shard_map/all_to_all | solution.py:249
  69.4 4.1 shard_map.152
  73.5 5.9 %all-to-all-start.2 = ((f32[256,2,128]{2,1,0:T(2,128)}), f32[256,2,128]{2,1,0:T(2,128)S(1)}, u32[]{:S(2)}, u32[]{:S(2)}) async-start(f32[256,2,128]{2,1,0:T(2,128)} %bitcast.71), calls=%async_computation.2 | async-start | bytes 524288 | tf_op jit(solution)/shard_map/all_to_all | solution.py:249
  79.4 4.7 %shard_map.153 = (f32[256,128]{1,0:T(8,128)}, f32[256,128]{1,0:T(8,128)}, f32[256,128]{1,0:T(8,128)}, f32[256,128]{1,0:T(8,128)}) custom-call(f32[512,128]{1,0:T(8,128)} %bitcast.66, bf16[2,512,256]{2,1,0:T(8,128)(2,1)} %constant.106.clone.refs_1_.refs_4_, f32[2,256,128]{2,1,0:T(8,128)} %constant.107.clone.refs_2_.refs_3_, ...), custom_call_target="tpu_custom_call" | custom-call | flops 1200000000 | bytes 2555904 | tf_op jit(solution)/shard_map/pallas_call | solution.py:234
  84.1 11.1 %all-to-all-done.2 = f32[256,2,128]{2,1,0:T(2,128)S(1)} async-done(((f32[256,2,128]{2,1,0:T(2,128)}), f32[256,2,128]{2,1,0:T(2,128)S(1)}, u32[]{:S(2)}, u32[]{:S(2)}) %all-to-all-start.2) | async-done | bytes 262176 | tf_op jit(solution)/shard_map/all_to_all | solution.py:249
  95.9 4.6 shard_map.154
  100.5 5.6 %all-to-all-start.3 = ((f32[256,4,128]{2,1,0:T(4,128)}), f32[256,4,128]{2,1,0:T(4,128)S(1)}, u32[]{:S(2)}, u32[]{:S(2)}) async-start(f32[256,4,128]{2,1,0:T(4,128)} %bitcast.62), calls=%async_computation.3 | async-start | bytes 1048576 | tf_op jit(solution)/shard_map/all_to_all | solution.py:249
  106.2 4.2 shard_map.155
  110.4 17.2 %all-to-all-done.3 = f32[256,4,128]{2,1,0:T(4,128)S(1)} async-done(((f32[256,4,128]{2,1,0:T(4,128)}), f32[256,4,128]{2,1,0:T(4,128)S(1)}, u32[]{:S(2)}, u32[]{:S(2)}) %all-to-all-start.3) | async-done | bytes 524320 | tf_op jit(solution)/shard_map/all_to_all | solution.py:249
  128.4 4.1 shard_map.156
  132.5 20.2 %all_to_all.80 = f32[256,1,128]{2,1,0:T(1,128)} all-to-all(f32[256,1,128]{2,1,0:T(1,128)} %bitcast.81), channel_id=1, replica_groups=mesh['rows'=64,'cols'=4] {'rows','cols'}, dimensions={0} | all-to-all | bytes 262144 | tf_op jit(solution)/shard_map/all_to_all | solution.py:249
  152.7 3.9 shard_map.157
  156.6 6.4 %all-to-all-start.5 = ((f32[256,4,128]{2,1,0:T(4,128)}), f32[256,4,128]{2,1,0:T(4,128)S(1)}, u32[]{:S(2)}, u32[]{:S(2)}) async-start(f32[256,4,128]{2,1,0:T(4,128)} %bitcast.60), calls=%async_computation.5 | async-start | bytes 1048576 | tf_op jit(solution)/shard_map/all_to_all | solution.py:249
  163.0 4.2 shard_map.158
  167.2 17.1 %all-to-all-done.5 = f32[256,4,128]{2,1,0:T(4,128)S(1)} async-done(((f32[256,4,128]{2,1,0:T(4,128)}), f32[256,4,128]{2,1,0:T(4,128)S(1)}, u32[]{:S(2)}, u32[]{:S(2)}) %all-to-all-start.5) | async-done | bytes 524320 | tf_op jit(solution)/shard_map/all_to_all | solution.py:249
  185.2 4.2 shard_map.159
  189.4 5.5 %all-to-all-start.6 = ((f32[256,1,128]{2,1,0:T(1,128)}), f32[256,1,128]{2,1,0:T(1,128)S(1)}, u32[]{:S(2)}, u32[]{:S(2)}) async-start(f32[256,1,128]{2,1,0:T(1,128)} %bitcast.79), calls=%async_computation.6 | async-start | bytes 262144 | tf_op jit(solution)/shard_map/all_to_all | solution.py:249
  194.9 4.2 shard_map.161
  199.1 8.8 %all-to-all-done.6 = f32[256,1,128]{2,1,0:T(1,128)S(1)} async-done(((f32[256,1,128]{2,1,0:T(1,128)}), f32[256,1,128]{2,1,0:T(1,128)S(1)}, u32[]{:S(2)}, u32[]{:S(2)}) %all-to-all-start.6) | async-done | bytes 131104 | tf_op jit(solution)/shard_map/all_to_all | solution.py:249
  208.6 3.8 shard_map.160
  212.4 6.1 %all-to-all-start.7 = ((f32[256,2,128]{2,1,0:T(2,128)}), f32[256,2,128]{2,1,0:T(2,128)S(1)}, u32[]{:S(2)}, u32[]{:S(2)}) async-start(f32[256,2,128]{2,1,0:T(2,128)} %bitcast.72), calls=%async_computation.7 | async-start | bytes 524288 | tf_op jit(solution)/shard_map/all_to_all | solution.py:249
  220.7 13.9 %all-to-all-done.7 = f32[256,2,128]{2,1,0:T(2,128)S(1)} async-done(((f32[256,2,128]{2,1,0:T(2,128)}), f32[256,2,128]{2,1,0:T(2,128)S(1)}, u32[]{:S(2)}, u32[]{:S(2)}) %all-to-all-start.7) | async-done | bytes 262176 | tf_op jit(solution)/shard_map/all_to_all | solution.py:249
  235.2 5.8 %shard_map.162 = (f32[512,128]{1,0:T(8,128)}, f32[256,256]{1,0:T(8,128)}, f32[256,256]{1,0:T(8,128)}) custom-call(f32[512,128]{1,0:T(8,128)} %bitcast.46, bf16[2,256,128]{2,1,0:T(8,128)(2,1)} %constant.111.clone.refs_1_, f32[2,256,512]{2,1,0:T(8,128)} %constant.104.clone.refs_2_, bf16[2,512,256]{2,1,0:T(8,128)(2,1)} %constant.112.clone.refs_3_, ...), custom_call_target="tpu_custom_call" | custom-call | flops 1800000000 | bytes 6029312 | tf_op jit(solution)/shard_map/pallas_call | solution.py:234
  241.0 23.0 %all_to_all.81 = f32[256,2,128]{2,1,0:T(2,128)} all-to-all(f32[256,2,128]{2,1,0:T(2,128)} %bitcast.73), channel_id=1, replica_groups=mesh['rows'=64,'cols'=4] {'rows','cols'}, dimensions={0} | all-to-all | bytes 524288 | tf_op jit(solution)/shard_map/all_to_all | solution.py:249
  264.0 3.7 shard_map.163
  267.7 5.7 %all-to-all-start.9 = ((f32[256,1,128]{2,1,0:T(1,128)}), f32[256,1,128]{2,1,0:T(1,128)S(1)}, u32[]{:S(2)}, u32[]{:S(2)}) async-start(f32[256,1,128]{2,1,0:T(1,128)} %bitcast.78), calls=%async_computation.9 | async-start | bytes 262144 | tf_op jit(solution)/shard_map/all_to_all | solution.py:249
  274.3 3.6 shard_map.164
  277.9 8.5 %all-to-all-done.9 = f32[256,1,128]{2,1,0:T(1,128)S(1)} async-done(((f32[256,1,128]{2,1,0:T(1,128)}), f32[256,1,128]{2,1,0:T(1,128)S(1)}, u32[]{:S(2)}, u32[]{:S(2)}) %all-to-all-start.9) | async-done | bytes 131104 | tf_op jit(solution)/shard_map/all_to_all | solution.py:249
  287.1 4.7 %shard_map.165 = (f32[1024,128]{1,0:T(8,128)}, f32[256,256]{1,0:T(8,128)}) custom-call(f32[256,128]{1,0:T(8,128)} %bitcast.74, bf16[2,256,128]{2,1,0:T(8,128)(2,1)} %constant.111.clone.refs_1_, f32[2,256,512]{2,1,0:T(8,128)} %constant.104.clone.refs_2_, bf16[2,512,256]{2,1,0:T(8,128)(2,1)} %constant.112.clone.refs_3_, ...), custom_call_target="tpu_custom_call" | custom-call | flops 1800000000 | bytes 5111808 | tf_op jit(solution)/shard_map/pallas_call | solution.py:234
  291.8 6.0 %all-to-all-start.10 = ((f32[256,4,128]{2,1,0:T(4,128)}), f32[256,4,128]{2,1,0:T(4,128)S(1)}, u32[]{:S(2)}, u32[]{:S(2)}) async-start(f32[256,4,128]{2,1,0:T(4,128)} %bitcast.55), calls=%async_computation.10 | async-start | bytes 1048576 | tf_op jit(solution)/shard_map/all_to_all | solution.py:249
  297.9 3.1 shard_map.169
  301.0 2.0 multiply_subtract_fusion.1
  303.0 3.6 shard_map.170
  306.7 2.7 shard_map.166.refs_7_.refs_6_
  309.4 9.9 %all-to-all-done.10 = f32[256,4,128]{2,1,0:T(4,128)S(1)} async-done(((f32[256,4,128]{2,1,0:T(4,128)}), f32[256,4,128]{2,1,0:T(4,128)S(1)}, u32[]{:S(2)}, u32[]{:S(2)}) %all-to-all-start.10) | async-done | bytes 524320 | tf_op jit(solution)/shard_map/all_to_all | solution.py:249
  320.1 3.8 shard_map.167
  323.9 6.0 %all-to-all-start.11 = ((f32[256,1,128]{2,1,0:T(1,128)}), f32[256,1,128]{2,1,0:T(1,128)S(1)}, u32[]{:S(2)}, u32[]{:S(2)}) async-start(f32[256,1,128]{2,1,0:T(1,128)} %bitcast.49), calls=%async_computation.11 | async-start | bytes 262144 | tf_op jit(solution)/shard_map/all_to_all | solution.py:249
  330.6 2.8 shard_map.168.refs_7_
  333.4 9.4 %all-to-all-done.11 = f32[256,1,128]{2,1,0:T(1,128)S(1)} async-done(((f32[256,1,128]{2,1,0:T(1,128)}), f32[256,1,128]{2,1,0:T(1,128)S(1)}, u32[]{:S(2)}, u32[]{:S(2)}) %all-to-all-start.11) | async-done | bytes 131104 | tf_op jit(solution)/shard_map/all_to_all | solution.py:249
  343.5 4.1 shard_map.171
  347.6 6.0 %all-to-all-start.12 = ((f32[256,4,128]{2,1,0:T(4,128)}), f32[256,4,128]{2,1,0:T(4,128)S(1)}, u32[]{:S(2)}, u32[]{:S(2)}) async-start(f32[256,4,128]{2,1,0:T(4,128)} %bitcast.59), calls=%async_computation.12 | async-start | bytes 1048576 | tf_op jit(solution)/shard_map/all_to_all | solution.py:249
  353.6 3.6 shard_map.175
  357.2 4.1 shard_map.172
  361.3 13.7 %all-to-all-done.12 = f32[256,4,128]{2,1,0:T(4,128)S(1)} async-done(((f32[256,4,128]{2,1,0:T(4,128)}), f32[256,4,128]{2,1,0:T(4,128)S(1)}, u32[]{:S(2)}, u32[]{:S(2)}) %all-to-all-start.12) | async-done | bytes 524320 | tf_op jit(solution)/shard_map/all_to_all | solution.py:249
  375.8 4.1 shard_map.173
  380.0 5.6 %all-to-all-start.13 = ((f32[256,1,128]{2,1,0:T(1,128)}), f32[256,1,128]{2,1,0:T(1,128)S(1)}, u32[]{:S(2)}, u32[]{:S(2)}) async-start(f32[256,1,128]{2,1,0:T(1,128)} %bitcast.48), calls=%async_computation.13 | async-start | bytes 262144 | tf_op jit(solution)/shard_map/all_to_all | solution.py:249
  386.4 2.8 shard_map.174.refs_7_
  389.2 9.4 %all-to-all-done.13 = f32[256,1,128]{2,1,0:T(1,128)S(1)} async-done(((f32[256,1,128]{2,1,0:T(1,128)}), f32[256,1,128]{2,1,0:T(1,128)S(1)}, u32[]{:S(2)}, u32[]{:S(2)}) %all-to-all-start.13) | async-done | bytes 131104 | tf_op jit(solution)/shard_map/all_to_all | solution.py:249
  399.3 4.1 shard_map.176
  403.4 6.3 %all-to-all-start.14 = ((f32[256,4,128]{2,1,0:T(4,128)}), f32[256,4,128]{2,1,0:T(4,128)S(1)}, u32[]{:S(2)}, u32[]{:S(2)}) async-start(f32[256,4,128]{2,1,0:T(4,128)} %bitcast.56), calls=%async_computation.14 | async-start | bytes 1048576 | tf_op jit(solution)/shard_map/all_to_all | solution.py:249
  409.8 2.7 shard_map.177.refs_9_
  412.4 4.6 shard_map.178
  417.0 2.9 shard_map.179.refs_8_
  419.9 11.1 %all-to-all-done.14 = f32[256,4,128]{2,1,0:T(4,128)S(1)} async-done(((f32[256,4,128]{2,1,0:T(4,128)}), f32[256,4,128]{2,1,0:T(4,128)S(1)}, u32[]{:S(2)}, u32[]{:S(2)}) %all-to-all-start.14) | async-done | bytes 524320 | tf_op jit(solution)/shard_map/all_to_all | solution.py:249
  431.9 6.2 %shard_map.180 = f32[512,128]{1,0:T(8,128)} custom-call(f32[1024,128]{1,0:T(8,128)} %bitcast.52, bf16[2,512,256]{2,1,0:T(8,128)(2,1)} %constant.106.clone.refs_1_.refs_4_, f32[2,256,128]{2,1,0:T(8,128)} %constant.107.clone.refs_2_.refs_3_, bf16[2,128,64]{2,1,0:T(8,128)(2,1)} %constant.108.clone.refs_3_, bf16[2,64,128]{2,1,0:T(8,128)(2,1)} %constant.109.clone.refs_4_.refs_1_, ...), custom_call_target="tpu_custom_call" | custom-call | flops 1200000000 | bytes 2752512 | tf_op jit(solution)/shard_map/pallas_call | solution.py:234
  438.1 7.3 %all-to-all-start.15 = ((f32[256,2,128]{2,1,0:T(2,128)}), f32[256,2,128]{2,1,0:T(2,128)}, u32[]{:S(2)}, u32[]{:S(2)}) async-start(f32[256,2,128]{2,1,0:T(2,128)} %bitcast.70), calls=%async_computation.15 | async-start | bytes 524288 | tf_op jit(solution)/shard_map/all_to_all | solution.py:249
  447.4 12.9 %all-to-all-done.15 = f32[256,2,128]{2,1,0:T(2,128)} async-done(((f32[256,2,128]{2,1,0:T(2,128)}), f32[256,2,128]{2,1,0:T(2,128)}, u32[]{:S(2)}, u32[]{:S(2)}) %all-to-all-start.15) | async-done | bytes 262176 | tf_op jit(solution)/shard_map/all_to_all | solution.py:249
  460.4 4.3 shard_map.181
  (90 shorter events, 16.9 us)
Async XLA Ops:
  4.6 31.5 %all-to-all-start = ((f32[256,2,128]{2,1,0:T(2,128)}), f32[256,2,128]{2,1,0:T(2,128)S(1)}, u32[]{:S(2)}, u32[]{:S(2)}) async-start(f32[256,2,128]{2,1,0:T(2,128)} %bitcast.69), calls=%async_computation | async-start | bytes 524288 | tf_op jit(solution)/shard_map/all_to_all | solution.py:249
  36.1 0.7 copy-start.31
  41.4 27.1 %all-to-all-start.1 = ((f32[256,4,128]{2,1,0:T(4,128)}), f32[256,4,128]{2,1,0:T(4,128)S(1)}, u32[]{:S(2)}, u32[]{:S(2)}) async-start(f32[256,4,128]{2,1,0:T(4,128)} %bitcast.61), calls=%async_computation.1 | async-start | bytes 1048576 | tf_op jit(solution)/shard_map/all_to_all | solution.py:249
  68.6 0.8 copy-start.26
  73.5 21.7 %all-to-all-start.2 = ((f32[256,2,128]{2,1,0:T(2,128)}), f32[256,2,128]{2,1,0:T(2,128)S(1)}, u32[]{:S(2)}, u32[]{:S(2)}) async-start(f32[256,2,128]{2,1,0:T(2,128)} %bitcast.71), calls=%async_computation.2 | async-start | bytes 524288 | tf_op jit(solution)/shard_map/all_to_all | solution.py:249
  95.2 0.7 copy-start.30
  100.5 27.1 %all-to-all-start.3 = ((f32[256,4,128]{2,1,0:T(4,128)}), f32[256,4,128]{2,1,0:T(4,128)S(1)}, u32[]{:S(2)}, u32[]{:S(2)}) async-start(f32[256,4,128]{2,1,0:T(4,128)} %bitcast.62), calls=%async_computation.3 | async-start | bytes 1048576 | tf_op jit(solution)/shard_map/all_to_all | solution.py:249
  127.6 0.8 copy-start.28
  156.6 27.8 %all-to-all-start.5 = ((f32[256,4,128]{2,1,0:T(4,128)}), f32[256,4,128]{2,1,0:T(4,128)S(1)}, u32[]{:S(2)}, u32[]{:S(2)}) async-start(f32[256,4,128]{2,1,0:T(4,128)} %bitcast.60), calls=%async_computation.5 | async-start | bytes 1048576 | tf_op jit(solution)/shard_map/all_to_all | solution.py:249
  184.4 0.8 copy-start.29
  189.4 18.6 %all-to-all-start.6 = ((f32[256,1,128]{2,1,0:T(1,128)}), f32[256,1,128]{2,1,0:T(1,128)S(1)}, u32[]{:S(2)}, u32[]{:S(2)}) async-start(f32[256,1,128]{2,1,0:T(1,128)} %bitcast.79), calls=%async_computation.6 | async-start | bytes 262144 | tf_op jit(solution)/shard_map/all_to_all | solution.py:249
  207.9 0.6 copy-start.38
  208.6 10.0 %copy-start.24 = (f32[256,256]{1,0:T(8,128)S(1)}, f32[256,256]{1,0:T(8,128)}, u32[]{:S(2)}) copy-start(f32[256,256]{1,0:T(8,128)} %get-tuple-element.72) | copy-start | bytes 786436
  208.6 10.0 %copy-start.25 = (f32[256,256]{1,0:T(8,128)S(1)}, f32[256,256]{1,0:T(8,128)}, u32[]{:S(2)}) copy-start(f32[256,256]{1,0:T(8,128)} %get-tuple-element.73) | copy-start | bytes 786436
  208.6 10.8 %copy-start.16 = (f32[256,256]{1,0:T(8,128)S(1)}, f32[256,256]{1,0:T(8,128)}, u32[]{:S(2)}) copy-start(f32[256,256]{1,0:T(8,128)} %get-tuple-element.67) | copy-start | bytes 786436
  208.6 10.8 %copy-start.17 = (f32[256,256]{1,0:T(8,128)S(1)}, f32[256,256]{1,0:T(8,128)}, u32[]{:S(2)}) copy-start(f32[256,256]{1,0:T(8,128)} %get-tuple-element.62.refs_7_) | copy-start | bytes 786436
  208.6 10.8 %copy-start.19 = (f32[256,256]{1,0:T(8,128)S(1)}, f32[256,256]{1,0:T(8,128)}, u32[]{:S(2)}) copy-start(f32[256,256]{1,0:T(8,128)} %get-tuple-element.70) | copy-start | bytes 786436
  208.6 10.8 %copy-start.21 = (f32[256,256]{1,0:T(8,128)S(1)}, f32[256,256]{1,0:T(8,128)}, u32[]{:S(2)}) copy-start(f32[256,256]{1,0:T(8,128)} %get-tuple-element.68) | copy-start | bytes 786436
  208.6 10.8 %copy-start.23 = (f32[256,256]{1,0:T(8,128)S(1)}, f32[256,256]{1,0:T(8,128)}, u32[]{:S(2)}) copy-start(f32[256,256]{1,0:T(8,128)} %get-tuple-element.69) | copy-start | bytes 786436
  212.4 7.0 %copy-start.14 = (f32[256,256]{1,0:T(8,128)S(1)}, f32[256,256]{1,0:T(8,128)}, u32[]{:S(2)}) copy-start(f32[256,256]{1,0:T(8,128)} %get-tuple-element.63.refs_8_) | copy-start | bytes 786436
  212.4 7.0 %copy-start.15 = (f32[256,256]{1,0:T(8,128)S(1)}, f32[256,256]{1,0:T(8,128)}, u32[]{:S(2)}) copy-start(f32[256,256]{1,0:T(8,128)} %get-tuple-element.71) | copy-start | bytes 786436
  212.4 22.1 %all-to-all-start.7 = ((f32[256,2,128]{2,1,0:T(2,128)}), f32[256,2,128]{2,1,0:T(2,128)S(1)}, u32[]{:S(2)}, u32[]{:S(2)}) async-start(f32[256,2,128]{2,1,0:T(2,128)} %bitcast.72), calls=%async_computation.7 | async-start | bytes 524288 | tf_op jit(solution)/shard_map/all_to_all | solution.py:249
  218.6 1.0 copy-start
  218.6 1.1 copy-start.12
  218.6 1.2 copy-start.13
  234.5 0.7 copy-start.9
  264.0 9.4 %copy-start.10 = (f32[256,256]{1,0:T(8,128)S(1)}, f32[256,256]{1,0:T(8,128)}, u32[]{:S(2)}) copy-start(f32[256,256]{1,0:T(8,128)} %get-tuple-element.78) | copy-start | bytes 786436
  267.7 5.7 %copy-start.1 = (f32[256,256]{1,0:T(8,128)S(1)}, f32[256,256]{1,0:T(8,128)}, u32[]{:S(2)}) copy-start(f32[256,256]{1,0:T(8,128)} %get-tuple-element.53.refs_6_.refs_10_) | copy-start | bytes 786436
  267.7 18.7 %all-to-all-start.9 = ((f32[256,1,128]{2,1,0:T(1,128)}), f32[256,1,128]{2,1,0:T(1,128)S(1)}, u32[]{:S(2)}, u32[]{:S(2)}) async-start(f32[256,1,128]{2,1,0:T(1,128)} %bitcast.78), calls=%async_computation.9 | async-start | bytes 262144 | tf_op jit(solution)/shard_map/all_to_all | solution.py:249
  286.4 0.7 copy-start.35
  291.8 27.5 %all-to-all-start.10 = ((f32[256,4,128]{2,1,0:T(4,128)}), f32[256,4,128]{2,1,0:T(4,128)S(1)}, u32[]{:S(2)}, u32[]{:S(2)}) async-start(f32[256,4,128]{2,1,0:T(4,128)} %bitcast.55), calls=%async_computation.10 | async-start | bytes 1048576 | tf_op jit(solution)/shard_map/all_to_all | solution.py:249
  297.8 3.1 copy-start.11
  297.8 3.1 copy-start.32
  297.8 3.1 copy-start.33
  297.8 3.1 copy-start.34
  319.3 0.8 copy-start.6
  320.1 9.8 %copy-start.7 = (f32[256,256]{1,0:T(8,128)S(1)}, f32[256,256]{1,0:T(8,128)}, u32[]{:S(2)}) copy-start(f32[256,256]{1,0:T(8,128)} %get-tuple-element.83) | copy-start | bytes 786436
  323.9 6.0 %copy-start.2 = (f32[256,256]{1,0:T(8,128)S(1)}, f32[256,256]{1,0:T(8,128)}, u32[]{:S(2)}) copy-start(f32[256,256]{1,0:T(8,128)} %get-tuple-element.53.refs_6_.refs_10_) | copy-start | bytes 786436
  323.9 18.9 %all-to-all-start.11 = ((f32[256,1,128]{2,1,0:T(1,128)}), f32[256,1,128]{2,1,0:T(1,128)S(1)}, u32[]{:S(2)}, u32[]{:S(2)}) async-start(f32[256,1,128]{2,1,0:T(1,128)} %bitcast.49), calls=%async_computation.11 | async-start | bytes 262144 | tf_op jit(solution)/shard_map/all_to_all | solution.py:249
  342.8 0.7 copy-start.37
  347.6 27.4 %all-to-all-start.12 = ((f32[256,4,128]{2,1,0:T(4,128)}), f32[256,4,128]{2,1,0:T(4,128)S(1)}, u32[]{:S(2)}, u32[]{:S(2)}) async-start(f32[256,4,128]{2,1,0:T(4,128)} %bitcast.59), calls=%async_computation.12 | async-start | bytes 1048576 | tf_op jit(solution)/shard_map/all_to_all | solution.py:249
  375.0 0.8 copy-start.5
  375.8 9.8 %copy-start.8 = (f32[256,256]{1,0:T(8,128)S(1)}, f32[256,256]{1,0:T(8,128)}, u32[]{:S(2)}) copy-start(f32[256,256]{1,0:T(8,128)} %get-tuple-element.91) | copy-start | bytes 786436
  380.0 5.7 %copy-start.3 = (f32[256,256]{1,0:T(8,128)S(1)}, f32[256,256]{1,0:T(8,128)}, u32[]{:S(2)}) copy-start(f32[256,256]{1,0:T(8,128)} %get-tuple-element.53.refs_6_.refs_10_) | copy-start | bytes 786436
  380.0 18.6 %all-to-all-start.13 = ((f32[256,1,128]{2,1,0:T(1,128)}), f32[256,1,128]{2,1,0:T(1,128)S(1)}, u32[]{:S(2)}, u32[]{:S(2)}) async-start(f32[256,1,128]{2,1,0:T(1,128)} %bitcast.48), calls=%async_computation.13 | async-start | bytes 262144 | tf_op jit(solution)/shard_map/all_to_all | solution.py:249
  398.6 0.7 copy-start.36
  403.4 27.7 %all-to-all-start.14 = ((f32[256,4,128]{2,1,0:T(4,128)}), f32[256,4,128]{2,1,0:T(4,128)S(1)}, u32[]{:S(2)}, u32[]{:S(2)}) async-start(f32[256,4,128]{2,1,0:T(4,128)} %bitcast.56), calls=%async_computation.14 | async-start | bytes 1048576 | tf_op jit(solution)/shard_map/all_to_all | solution.py:249
  431.1 0.8 copy-start.27
  431.9 13.5 %copy-start.20 = (f32[256,256]{1,0:T(8,128)S(1)}, f32[256,256]{1,0:T(8,128)}, u32[]{:S(2)}) copy-start(f32[256,256]{1,0:T(8,128)} %get-tuple-element.70) | copy-start | bytes 786436
  431.9 13.5 %copy-start.22 = (f32[256,256]{1,0:T(8,128)S(1)}, f32[256,256]{1,0:T(8,128)}, u32[]{:S(2)}) copy-start(f32[256,256]{1,0:T(8,128)} %get-tuple-element.68) | copy-start | bytes 786436
  438.1 7.4 %copy-start.4 = (f32[256,256]{1,0:T(8,128)S(1)}, f32[256,256]{1,0:T(8,128)}, u32[]{:S(2)}) copy-start(f32[256,256]{1,0:T(8,128)} %get-tuple-element.53.refs_6_.refs_10_) | copy-start | bytes 786436
  438.1 7.4 %copy-start.18 = (f32[256,256]{1,0:T(8,128)S(1)}, f32[256,256]{1,0:T(8,128)}, u32[]{:S(2)}) copy-start(f32[256,256]{1,0:T(8,128)} %get-tuple-element.62.refs_7_) | copy-start | bytes 786436
  438.1 22.3 %all-to-all-start.15 = ((f32[256,2,128]{2,1,0:T(2,128)}), f32[256,2,128]{2,1,0:T(2,128)}, u32[]{:S(2)}, u32[]{:S(2)}) async-start(f32[256,2,128]{2,1,0:T(2,128)} %bitcast.70), calls=%async_computation.15 | async-start | bytes 524288 | tf_op jit(solution)/shard_map/all_to_all | solution.py:249
where the time goes:
time: 473 us; the launch traced here: 465 us
  waiting for transfers between devices  176 us (37%)
  Pallas kernels  131 us (28%)
  starting transfers between devices  93.9 us (20%)
  blocking collectives  43.2 us (9%)
  local copies, waits for them, and re-layouts  9.99 us (2%)
  other arithmetic  8.99 us (2%)
    all_to_all x14, waiting for transfers between devices, exchange(): lax.all_to_all(values, mesh_axes, split_axis=0, concat_axis=0, tiled=True)  176 us
    pallas_call x33, Pallas kernels, run(): pl.pallas_call(kernel, out_shape=list(outputs), in_specs=[outside] * tota...  131 us
    all_to_all x14, starting transfers between devices, exchange(): lax.all_to_all(values, mesh_axes, split_axis=0, concat_axis=0, tiled=True)  93.9 us
    all_to_all x2, blocking collectives, exchange(): lax.all_to_all(values, mesh_axes, split_axis=0, concat_axis=0, tiled=True)  43.2 us
    unnamed x78, local copies, waits for them, and re-layouts  9.98 us
  transfers between devices with their start and end apart: 14, of which 14 were waited for; matrix products, arithmetic and copies ran while one was open for 2% of the time, Pallas kernels for 12%

commit v1 on v0

--- a/solution.py
+++ b/solution.py
@@ -175,11 +175,12 @@
 
 
 def message(count):
-    return jax.ShapeDtypeStruct((devices * count, 128), jnp.float32)
-
-
-field_shape = jax.ShapeDtypeStruct((256, 256), jnp.float32)
-spectrum_shape = jax.ShapeDtypeStruct((fine, 64), jnp.float32)
+    return pltpu.HBM((devices * count, 128), jnp.float32)
+
+
+part_shape = pltpu.HBM((devices, 128), jnp.float32)
+field_shape = pltpu.HBM((256, 256), jnp.float32)
+spectrum_shape = pltpu.HBM((fine, 64), jnp.float32)
 
 
 class Fetched:
@@ -199,46 +200,102 @@
         return self.target[index]
 
 
-def run(body, names, inputs, outputs, flops):
-    operands = [inputs[0]] + [jnp.asarray(tables()[name]) for name in names] + list(inputs[1:])
+def is_near(shape):
+    return shape.memory_space == pltpu.VMEM
+
+
+resident_names = ("left_x", "twist_x", "right_x", "right_x_back", "twist_y", "left_y_back")
+
+
+def stage_tables():
+    names = resident_names
+    values = [pltpu.with_memory_space_constraint(jnp.asarray(tables()[name]), pltpu.HBM) for name in names]
+    count = len(values)
+
+    def kernel(*refs):
+        copies = [
+            pltpu.make_async_copy(refs[i], refs[count + i], refs[-1].at[i]) for i in range(count)
+        ]
+        for copy in copies:
+            copy.start()
+        for copy in copies:
+            copy.wait()
+
+    staged = pl.pallas_call(
+        kernel,
+        out_shape=[pltpu.VMEM(a.shape, a.dtype) for a in values],
+        in_specs=[pl.BlockSpec(memory_space=pltpu.HBM)] * count,
+        out_specs=[pl.BlockSpec(memory_space=pltpu.VMEM)] * count,
+        scratch_shapes=[pltpu.SemaphoreType.DMA((count,))],
+        compiler_params=pltpu.CompilerParams(vmem_limit_bytes=vmem_limit),
+        cost_estimate=pl.CostEstimate(flops=0, bytes_accessed=8_000_000, transcendentals=0),
+    )(*values)
+    return dict(zip(names, staged))
+
+
+vmem_limit = 24_000_000
+
+
+def run(staged, body, names, inputs, outputs, flops):
+    staged = staged or {}
+    operands = [inputs[0]] + [
+        staged[name] if name in staged else jnp.asarray(tables()[name]) for name in names
+    ]
+    operands = operands + list(inputs[1:])
+    near = {1 + place for place, name in enumerate(names) if name in staged}
+    near = near | ({0} if inputs[0].shape[1] == 128 else set())
+    far = set(range(len(operands))) - near
+    operands = [
+        pltpu.with_memory_space_constraint(a, pltpu.HBM if place in far else pltpu.VMEM)
+        for place, a in enumerate(operands)
+    ]
     total_in = len(operands)
     total = total_in + len(outputs)
+    moving = sorted(far)
+    leaving = [place for place, shape in enumerate(outputs) if not is_near(shape)]
 
     def kernel(*refs):
         semaphores = refs[-1]
         held = refs[total:-1]
-        fetched = [Fetched(refs[i], held[i], semaphores.at[i]) for i in range(total_in)]
+        fetched = list(refs[:total_in])
+        for slot, place in enumerate(moving):
+            fetched[place] = Fetched(refs[place], held[slot], semaphores.at[place])
         tab = dict(zip(names, fetched[1 : 1 + len(names)]))
         ins = fetched[:1] + fetched[1 + len(names) :]
-        outs = held[total_in:]
+        outs = list(refs[total_in:total])
+        for slot, place in enumerate(leaving):
+            outs[place] = held[len(moving) + slot]
         sends = {}
 
         def emit(place):
-            copy = pltpu.make_async_copy(
-                outs[place], refs[total_in + place], semaphores.at[total_in + place]
-            )
-            copy.start()
-            sends[place] = copy
+            if place in leaving:
+                copy = pltpu.make_async_copy(
+                    outs[place], refs[total_in + place], semaphores.at[total_in + place]
+                )
+                copy.start()
+                sends[place] = copy
 
         body(tab, ins, outs, emit)
         for place in range(len(outs)):
             if place not in sends:
                 emit(place)
-        for item in fetched:
-            item.arrive()
+        for place in moving:
+            fetched[place].arrive()
         for copy in sends.values():
             copy.wait()
 
     outside = pl.BlockSpec(memory_space=pltpu.HBM)
+    inside = pl.BlockSpec(memory_space=pltpu.VMEM)
     moved = sum(4 * int(np.prod(a.shape)) for a in list(operands) + list(outputs))
+    scratch = [operands[place] for place in moving] + [outputs[place] for place in leaving]
     return pl.pallas_call(
         kernel,
         out_shape=list(outputs),
-        in_specs=[outside] * total_in,
-        out_specs=[outside] * len(outputs),
-        scratch_shapes=[pltpu.VMEM(a.shape, a.dtype) for a in list(operands) + list(outputs)]
+        in_specs=[outside if place in far else inside for place in range(total_in)],
+        out_specs=[inside if is_near(shape) else outside for shape in outputs],
+        scratch_shapes=[pltpu.VMEM(a.shape, a.dtype) for a in scratch]
         + [pltpu.SemaphoreType.DMA((total,))],
-        compiler_params=pltpu.CompilerParams(vmem_limit_bytes=60_000_000),
+        compiler_params=pltpu.CompilerParams(vmem_limit_bytes=vmem_limit),
         cost_estimate=pl.CostEstimate(flops=int(flops * 6e8), bytes_accessed=int(moved), transcendentals=0),
     )(*operands)
 
@@ -274,11 +331,11 @@
     weight = jnp.where(mode_y == 0, 1.0, 2.0)[None, :] / (side * side)
     keep = jnp.where(jnp.abs(mode_x) < side // 4, weight, 0.0).astype(jnp.float32)
     magnitude = jnp.sqrt(wave_x * wave_x + wave_y * wave_y)
-    return jnp.stack((keep, magnitude, wave_x, wave_y), 0)
+    return (jnp.stack((keep, magnitude), 0), jnp.stack((wave_x, wave_y), 0))
 
 
 def per_device(elevation, potential, elevation_cot, potential_cot):
-    waves = wave_tables()
+    waves, turns = wave_tables()
 
     def start(tab, ins, outs, emit):
         surface = gather_rows(ins[0][...])
@@ -287,8 +344,9 @@
         y_forward(tab, gather_rows(ins[1][...]), outs[1], 1, 2)
         y_forward(tab, surface, outs[1], 0, 2)
 
-    elev, sent = run(start, y_in, (elevation, potential), (field_shape, message(2)), 2)
+    elev, sent = run(None, start, y_in, (elevation, potential), (field_shape, message(2)), 2)
     first = exchange(sent)
+    staged = stage_tables()
 
     def cotangents(tab, ins, outs, emit):
         outs[0][...] = section_step * gather_rows(ins[0][...])
@@ -297,7 +355,7 @@
         y_forward(tab, -stiffness * rate, outs[2], 0, 1)
 
     rate_elev, rate_pot, bend_sent = run(
-        cotangents, y_in, (elevation_cot, potential_cot), (field_shape, field_shape, message(1)), 1
+        staged, cotangents, y_in, (elevation_cot, potential_cot), (field_shape, field_shape, part_shape), 1
     )
 
     def second(tab, ins, outs, emit):
@@ -308,19 +366,19 @@
             spec = spec * ins[1][1]
             x_inverse(tab, spec, None, outs[0], degree, 4)
 
-    sent, pot_spec = run(second, x_both, (first, waves), (message(4), spectrum_shape), 2)
+    sent, pot_spec = run(staged, second, x_both, (first, waves), (message(4), spectrum_shape), 2)
     lifts = exchange(sent)
 
     def slopes(tab, ins, outs, emit):
         spec = x_forward(tab, ins[0], 0, 2) * ins[2][0]
-        x_inverse(tab, None, spec * ins[2][2], outs[0], 0, 1)
-        x_inverse(tab, None, spec * ins[2][3], outs[1], 0, 1)
+        x_inverse(tab, None, spec * ins[3][0], outs[0], 0, 1)
+        x_inverse(tab, None, spec * ins[3][1], outs[1], 0, 1)
         spec = ins[1][...]
-        x_inverse(tab, None, spec * ins[2][2], outs[2], 0, 1)
-        x_inverse(tab, None, spec * ins[2][3], outs[3], 0, 1)
+        x_inverse(tab, None, spec * ins[3][0], outs[2], 0, 1)
+        x_inverse(tab, None, spec * ins[3][1], outs[3], 0, 1)
 
     slope_x_sent, slope_y_sent, flow_x_sent, flow_y_sent = run(
-        slopes, x_turn, (first, pot_spec, waves), (message(1),) * 4, 2
+        staged, slopes, x_turn, (first, pot_spec, waves, turns), (part_shape,) * 4, 2
     )
 
     def third(tab, ins, outs, emit):
@@ -330,7 +388,7 @@
         y_forward(tab, -ins[1][...] * lifted, outs[0], 0, 2)
         put(outs[0], ins[2][...], 1, 2)
 
-    sent, lift_11 = run(third, y_both, (lifts, elev, bend_sent), (message(2), field_shape), 2)
+    sent, lift_11 = run(staged, third, y_both, (lifts, elev, bend_sent), (message(2), field_shape), 2)
     arrived = exchange(sent)
 
     def inverse_of(slots, count):
@@ -341,7 +399,7 @@
 
         return body
 
-    lift_12, lift_13, lift_14 = run(inverse_of((1, 2, 3), 4), y_out, (lifts,), (field_shape,) * 3, 3)
+    lift_12, lift_13, lift_14 = run(staged, inverse_of((1, 2, 3), 4), y_out, (lifts,), (field_shape,) * 3, 3)
 
     def fourth(tab, ins, outs, emit):
         spec = x_forward(tab, ins[0], 0, 2) * ins[1][0]
@@ -350,7 +408,7 @@
             x_inverse(tab, spec, None, outs[0], degree, 4)
         put(outs[0], ins[2][...], 3, 4)
 
-    (sent,) = run(fourth, x_both, (arrived, waves, slope_x_sent), (message(4),), 2)
+    (sent,) = run(staged, fourth, x_both, (arrived, waves, slope_x_sent), (message(4),), 2)
 
     def spectra_of(slots, count):
         def body(tab, ins, outs, emit):
@@ -359,7 +417,7 @@
 
         return body
 
-    (bend_spec,) = run(spectra_of((1,), 2), x_in, (arrived, waves), (spectrum_shape,), 1)
+    (bend_spec,) = run(staged, spectra_of((1,), 2), x_in, (arrived, waves), (spectrum_shape,), 1)
     arrived = exchange(sent)
 
     def fifth(tab, ins, outs, emit):
@@ -369,8 +427,8 @@
         surface = ins[1][...]
         y_forward(tab, -surface * lifted - (surface * surface / 2.0) * ins[2][...], outs[0], 0, 1)
 
-    sent, lift_21 = run(fifth, y_both, (arrived, elev, lift_12), (message(1), field_shape), 2)
-    lift_22, lift_23, slope_x = run(inverse_of((1, 2, 3), 4), y_out, (arrived,), (field_shape,) * 3, 3)
+    sent, lift_21 = run(staged, fifth, y_both, (arrived, elev, lift_12), (message(1), field_shape), 2)
+    lift_22, lift_23, slope_x = run(staged, inverse_of((1, 2, 3), 4), y_out, (arrived,), (field_shape,) * 3, 3)
     arrived = exchange(sent)
 
     def sixth(tab, ins, outs, emit):
@@ -381,7 +439,7 @@
         put(outs[0], ins[2][...], 2, 4)
         put(outs[0], ins[3][...], 3, 4)
 
-    (sent,) = run(sixth, x_both, (arrived, waves, slope_y_sent, flow_x_sent), (message(4),), 2)
+    (sent,) = run(staged, sixth, x_both, (arrived, waves, slope_y_sent, flow_x_sent), (message(4),), 2)
     arrived = exchange(sent)
 
     def seventh(tab, ins, outs, emit):
@@ -393,8 +451,8 @@
         cube = square * surface / 3.0
         y_forward(tab, -surface * lifted - square * ins[2][...] - cube * ins[3][...], outs[0], 0, 1)
 
-    sent, lift_31 = run(seventh, y_both, (arrived, elev, lift_22, lift_13), (message(1), field_shape), 2)
-    lift_32, slope_y, flow_x = run(inverse_of((1, 2, 3), 4), y_out, (arrived,), (field_shape,) * 3, 3)
+    sent, lift_31 = run(staged, seventh, y_both, (arrived, elev, lift_22, lift_13), (message(1), field_shape), 2)
+    lift_32, slope_y, flow_x = run(staged, inverse_of((1, 2, 3), 4), y_out, (arrived,), (field_shape,) * 3, 3)
     arrived = exchange(sent)
 
     def eighth(tab, ins, outs, emit):
@@ -402,7 +460,7 @@
         x_inverse(tab, spec, None, outs[0], 0, 2)
         put(outs[0], ins[2][...], 1, 2)
 
-    (sent,) = run(eighth, x_both, (arrived, waves, flow_y_sent), (message(2),), 1)
+    (sent,) = run(staged, eighth, x_both, (arrived, waves, flow_y_sent), (message(2),), 1)
     arrived = exchange(sent)
 
     square = elev * elev / 2.0
@@ -429,13 +487,13 @@
         y_forward(tab, ins[5][...] * vertical_cot, outs[0], 1, 2)
 
     sent, vertical, vertical_cot = run(
-        ninth,
+        staged, ninth,
         y_both,
         (arrived, partial, steepness, rate_elev, rate_pot, elev),
         (message(2), field_shape, field_shape),
         3,
     )
-    (flow_y,) = run(inverse_of((1,), 2), y_out, (arrived,), (field_shape,), 1)
+    (flow_y,) = run(staged, inverse_of((1,), 2), y_out, (arrived,), (field_shape,), 1)
     arrived = exchange(sent)
     steep_cot = vertical * rate_elev + 0.5 * vertical * vertical * rate_pot
 
@@ -445,7 +503,7 @@
             emit(place)
 
     def sends_of(*fields):
-        return run(forward_all, y_in, fields, (message(1),) * len(fields), len(fields))
+        return run(staged, forward_all, y_in, fields, (part_shape,) * len(fields), len(fields))
 
     square_cot_sent, cube_cot_sent = sends_of(square * vertical_cot, cube * vertical_cot)
     slope_x_cot, slope_y_cot = sends_of(
@@ -461,8 +519,8 @@
         emit(1)
         x_inverse(tab, spec * ins[1][1], None, outs[0], 0, 1)
 
-    sent, cot_spec = run(tenth, x_both, (arrived, waves), (message(1), spectrum_shape), 1)
-    (elev_cot_spec,) = run(spectra_of((1,), 2), x_in, (arrived, waves), (spectrum_shape,), 1)
+    sent, cot_spec = run(staged, tenth, x_both, (arrived, waves), (message(1), spectrum_shape), 1)
+    (elev_cot_spec,) = run(staged, spectra_of((1,), 2), x_in, (arrived, waves), (spectrum_shape,), 1)
     arrived = exchange(sent)
 
     def eleventh(tab, ins, outs, emit):
@@ -476,7 +534,7 @@
         put(outs[0], ins[3][...], 3, 4)
 
     sent, fourth_cot = run(
-        eleventh, y_both, (arrived, elev, square_cot_sent, cube_cot_sent), (message(4), field_shape), 3
+        staged, eleventh, y_both, (arrived, elev, square_cot_sent, cube_cot_sent), (message(4), field_shape), 3
     )
     (cube_fourth_sent,) = sends_of(cube * fourth_cot)
     arrived = exchange(sent)
@@ -486,9 +544,9 @@
         spec = ins[1][1] * ((ins[2][...] - spec) + ins[1][1] * ins[3][...])
         x_inverse(tab, spec, None, outs[0], 0, 1)
 
-    (sent,) = run(twelfth, x_both, (arrived, waves, cot_spec, elev_cot_spec), (message(1),), 1)
+    (sent,) = run(staged, twelfth, x_both, (arrived, waves, cot_spec, elev_cot_spec), (message(1),), 1)
     square_fourth_spec, square_cot_spec, cube_cot_spec = run(
-        spectra_of((1, 2, 3), 4), x_in, (arrived, waves), (spectrum_shape,) * 3, 1
+        staged, spectra_of((1, 2, 3), 4), x_in, (arrived, waves), (spectrum_shape,) * 3, 1
     )
     arrived = exchange(sent)
 
@@ -501,7 +559,7 @@
             put(outs[0], ins[1 + slot][...], slot, 4)
 
     sent, third_cot = run(
-        thirteenth,
+        staged, thirteenth,
         y_both,
         (arrived, elev, cube_fourth_sent, slope_x_cot, slope_y_cot),
         (message(4), field_shape),
@@ -519,7 +577,7 @@
         x_inverse(tab, spec, None, outs[0], 0, 1)
 
     (sent,) = run(
-        fourteenth,
+        staged, fourteenth,
         x_both,
         (arrived, waves, cot_spec, elev_cot_spec, square_fourth_spec, square_cot_spec),
         (message(1),),
@@ -535,13 +593,13 @@
         )
         slope_x_spec = x_forward(tab, ins[0], 2, 4) * ins[1][0]
         slope_y_spec = x_forward(tab, ins[0], 3, 4) * ins[1][0]
-        outs[1][...] = -(ins[1][2] * slope_x_spec + ins[1][3] * slope_y_spec)
+        outs[1][...] = -(ins[7][0] * slope_x_spec + ins[7][1] * slope_y_spec)
         outs[2][...] = ins[6][...] * (wave * wave) * (wave * wave)
 
     pot_part, elev_turn, elev_part = run(
-        gathered,
+        staged, gathered,
         x_in,
-        (arrived, waves, cot_spec, elev_cot_spec, square_cot_spec, cube_cot_spec, bend_spec),
+        (arrived, waves, cot_spec, elev_cot_spec, square_cot_spec, cube_cot_spec, bend_spec, turns),
         (spectrum_shape,) * 3,
         1,
     )
@@ -556,7 +614,7 @@
             put(outs[0], ins[1 + slot][...], slot, 4)
 
     sent, second_cot = run(
-        fifteenth,
+        staged, fifteenth,
         y_both,
         (arrived, elev, square_third_sent, flow_x_cot, flow_y_cot),
         (message(4), field_shape),
@@ -567,19 +625,19 @@
     def elevation_side(tab, ins, outs, emit):
         x_inverse(tab, ins[0][...], ins[1][...], outs[0], 0, 1)
 
-    (elev_sent,) = run(elevation_side, x_out, (elev_part, elev_turn), (message(1),), 1)
+    (elev_sent,) = run(staged, elevation_side, x_out, (elev_part, elev_turn), (part_shape,), 1)
 
     def sixteenth(tab, ins, outs, emit):
         wave = ins[1][1]
         keep = ins[1][0]
         first_part = x_forward(tab, ins[0], 0, 4) * keep
         second_part = x_forward(tab, ins[0], 1, 4) * keep
-        flow_part = x_forward(tab, ins[0], 2, 4) * ins[1][2] + x_forward(tab, ins[0], 3, 4) * ins[1][3]
+        flow_part = x_forward(tab, ins[0], 2, 4) * ins[4][0] + x_forward(tab, ins[0], 3, 4) * ins[4][1]
         straight = ins[2][...] - wave * (first_part + wave * second_part)
         x_inverse(tab, straight, -flow_part * keep, outs[0], 1, 2)
         put(outs[0], ins[3][...], 0, 2)
 
-    (sent,) = run(sixteenth, x_all, (arrived, waves, pot_part, elev_sent), (message(2),), 2)
+    (sent,) = run(staged, sixteenth, x_all, (arrived, waves, pot_part, elev_sent, turns), (message(2),), 2)
     arrived = exchange(sent)
 
     grad = (
@@ -595,9 +653,9 @@
         emit(1)
         scatter_rows(outs[0], ins[1][...] + y_inverse(tab, ins[0], 0, 2), ins[2])
 
-    block = jax.ShapeDtypeStruct(elevation.shape, jnp.float32)
+    block = pltpu.HBM(elevation.shape, jnp.float32)
     elevation_grad, potential_grad = run(
-        finish, y_out, (arrived, grad, elevation_cot, potential_cot), (block, block), 2
+        staged, finish, y_out, (arrived, grad, elevation_cot, potential_cot), (block, block), 2
     )
     return (elevation_grad, potential_grad)
 

time: 473 us -> 449 us (0.949)
  Pallas kernels: 131 us -> 113 us
  local copies, waits for them, and re-layouts: 9.99 us -> 0.09 us
  other arithmetic: 8.99 us -> 15.7 us
    pallas_call x33 -> x34, Pallas kernels: 131 us -> 113 us  [the longest x33 111 us: run(): pl.pallas_call(kernel, out_shape=list(outputs), in_specs=[outside if plac...]
    unnamed x78 -> x30, local copies, waits for them, and re-layouts: 9.98 us -> 0.08 us
  transfers between devices with their start and end apart: 14 -> 14, of which waited for: 14 -> 14; matrix products, arithmetic and copies ran while one was open for 2% -> 4% of each run, Pallas kernels for 12% -> 12%
where the time goes in v1:
time: 449 us; the launch traced here: 441 us
  waiting for transfers between devices  176 us (39%)
  Pallas kernels  113 us (25%)
  starting transfers between devices  92.6 us (21%)
  blocking collectives  41.4 us (9%)
  other arithmetic  15.7 us (3%)
    all_to_all x14, waiting for transfers between devices, exchange(): lax.all_to_all(values, mesh_axes, split_axis=0, concat_axis=0, tiled=True)  176 us
    pallas_call x33, Pallas kernels, run(): pl.pallas_call(kernel, out_shape=list(outputs), in_specs=[outside if plac...  111 us
    all_to_all x14, starting transfers between devices, exchange(): lax.all_to_all(values, mesh_axes, split_axis=0, concat_axis=0, tiled=True)  92.6 us
    all_to_all x2, blocking collectives, exchange(): lax.all_to_all(values, mesh_axes, split_axis=0, concat_axis=0, tiled=True)  41.4 us
  transfers between devices with their start and end apart: 14, of which 14 were waited for; matrix products, arithmetic and copies ran while one was open for 4% of the time, Pallas kernels for 12%

profile of v1, /device:TPU:1, one launch (start us, length us, event | category | flops | bytes accessed | tf_op | source)
XLA Modules:
  0.0 440.6 jit_solution(1359566675637419336)
XLA Ops:
  0.6 4.0 shard_map.149
  4.6 15.7 %all-to-all-start = ((f32[256,2,128]{2,1,0:T(2,128)}), f32[256,2,128]{2,1,0:T(2,128)S(1)}, u32[]{:S(2)}, u32[]{:S(2)}) async-start(f32[256,2,128]{2,1,0:T(2,128)} %bitcast.74), calls=%async_computation | async-start | bytes 524288 | tf_op jit(solution)/shard_map/all_to_all | solution.py:306
  22.7 13.4 %all-to-all-done = f32[256,2,128]{2,1,0:T(2,128)S(1)} async-done(((f32[256,2,128]{2,1,0:T(2,128)}), f32[256,2,128]{2,1,0:T(2,128)S(1)}, u32[]{:S(2)}, u32[]{:S(2)}) %all-to-all-start) | async-done | bytes 262176 | tf_op jit(solution)/shard_map/all_to_all | solution.py:306
  36.1 3.6 shard_map.151
  39.7 5.7 %all-to-all-start.1 = ((f32[256,4,128]{2,1,0:T(4,128)}), f32[256,4,128]{2,1,0:T(4,128)S(1)}, u32[]{:S(2)}, u32[]{:S(2)}) async-start(f32[256,4,128]{2,1,0:T(4,128)} %bitcast.72), calls=%async_computation.1 | async-start | bytes 1048576 | tf_op jit(solution)/shard_map/all_to_all | solution.py:306
  45.4 3.0 shard_map.152
  48.4 18.5 %all-to-all-done.1 = f32[256,4,128]{2,1,0:T(4,128)S(1)} async-done(((f32[256,4,128]{2,1,0:T(4,128)}), f32[256,4,128]{2,1,0:T(4,128)S(1)}, u32[]{:S(2)}, u32[]{:S(2)}) %all-to-all-start.1) | async-done | bytes 524320 | tf_op jit(solution)/shard_map/all_to_all | solution.py:306
  66.9 3.5 shard_map.153
  70.4 5.9 %all-to-all-start.2 = ((f32[256,2,128]{2,1,0:T(2,128)}), f32[256,2,128]{2,1,0:T(2,128)S(1)}, u32[]{:S(2)}, u32[]{:S(2)}) async-start(f32[256,2,128]{2,1,0:T(2,128)} %bitcast.76), calls=%async_computation.2 | async-start | bytes 524288 | tf_op jit(solution)/shard_map/all_to_all | solution.py:306
  77.0 4.4 shard_map.154
  81.4 10.8 %all-to-all-done.2 = f32[256,2,128]{2,1,0:T(2,128)S(1)} async-done(((f32[256,2,128]{2,1,0:T(2,128)}), f32[256,2,128]{2,1,0:T(2,128)S(1)}, u32[]{:S(2)}, u32[]{:S(2)}) %all-to-all-start.2) | async-done | bytes 262176 | tf_op jit(solution)/shard_map/all_to_all | solution.py:306
  92.1 3.4 shard_map.155
  95.6 5.7 %all-to-all-start.3 = ((f32[256,4,128]{2,1,0:T(4,128)}), f32[256,4,128]{2,1,0:T(4,128)S(1)}, u32[]{:S(2)}, u32[]{:S(2)}) async-start(f32[256,4,128]{2,1,0:T(4,128)} %bitcast.73), calls=%async_computation.3 | async-start | bytes 1048576 | tf_op jit(solution)/shard_map/all_to_all | solution.py:306
  101.2 3.4 shard_map.156
  104.6 18.1 %all-to-all-done.3 = f32[256,4,128]{2,1,0:T(4,128)S(1)} async-done(((f32[256,4,128]{2,1,0:T(4,128)}), f32[256,4,128]{2,1,0:T(4,128)S(1)}, u32[]{:S(2)}, u32[]{:S(2)}) %all-to-all-start.3) | async-done | bytes 524320 | tf_op jit(solution)/shard_map/all_to_all | solution.py:306
  122.7 3.5 shard_map.157
  126.2 19.0 %all_to_all.80 = f32[256,1,128]{2,1,0:T(1,128)S(1)} all-to-all(f32[256,1,128]{2,1,0:T(1,128)} %bitcast.82), channel_id=1, replica_groups=mesh['rows'=64,'cols'=4] {'rows','cols'}, dimensions={0} | all-to-all | bytes 262144 | tf_op jit(solution)/shard_map/all_to_all | solution.py:306
  145.2 2.8 shard_map.158
  148.0 6.5 %all-to-all-start.5 = ((f32[256,4,128]{2,1,0:T(4,128)}), f32[256,4,128]{2,1,0:T(4,128)S(1)}, u32[]{:S(2)}, u32[]{:S(2)}) async-start(f32[256,4,128]{2,1,0:T(4,128)} %bitcast.71), calls=%async_computation.5 | async-start | bytes 1048576 | tf_op jit(solution)/shard_map/all_to_all | solution.py:306
  154.6 3.4 shard_map.159
  158.0 17.9 %all-to-all-done.5 = f32[256,4,128]{2,1,0:T(4,128)S(1)} async-done(((f32[256,4,128]{2,1,0:T(4,128)}), f32[256,4,128]{2,1,0:T(4,128)S(1)}, u32[]{:S(2)}, u32[]{:S(2)}) %all-to-all-start.5) | async-done | bytes 524320 | tf_op jit(solution)/shard_map/all_to_all | solution.py:306
  175.9 3.6 shard_map.160
  179.5 5.5 %all-to-all-start.6 = ((f32[256,1,128]{2,1,0:T(1,128)}), f32[256,1,128]{2,1,0:T(1,128)S(1)}, u32[]{:S(2)}, u32[]{:S(2)}) async-start(f32[256,1,128]{2,1,0:T(1,128)} %bitcast.80), calls=%async_computation.6 | async-start | bytes 262144 | tf_op jit(solution)/shard_map/all_to_all | solution.py:306
  185.0 3.4 shard_map.162
  188.4 9.6 %all-to-all-done.6 = f32[256,1,128]{2,1,0:T(1,128)S(1)} async-done(((f32[256,1,128]{2,1,0:T(1,128)}), f32[256,1,128]{2,1,0:T(1,128)S(1)}, u32[]{:S(2)}, u32[]{:S(2)}) %all-to-all-start.6) | async-done | bytes 131104 | tf_op jit(solution)/shard_map/all_to_all | solution.py:306
  198.0 2.6 shard_map.161
  200.5 6.0 %all-to-all-start.7 = ((f32[256,2,128]{2,1,0:T(2,128)}), f32[256,2,128]{2,1,0:T(2,128)S(1)}, u32[]{:S(2)}, u32[]{:S(2)}) async-start(f32[256,2,128]{2,1,0:T(2,128)} %bitcast.77), calls=%async_computation.7 | async-start | bytes 524288 | tf_op jit(solution)/shard_map/all_to_all | solution.py:306
  208.4 2.3 multiply_add_fusion.3.refs_6_
  210.7 11.8 %all-to-all-done.7 = f32[256,2,128]{2,1,0:T(2,128)S(1)} async-done(((f32[256,2,128]{2,1,0:T(2,128)}), f32[256,2,128]{2,1,0:T(2,128)S(1)}, u32[]{:S(2)}, u32[]{:S(2)}) %all-to-all-start.7) | async-done | bytes 262176 | tf_op jit(solution)/shard_map/all_to_all | solution.py:306
  222.5 5.2 %shard_map.163 = (f32[512,128]{1,0:T(8,128)}, f32[256,256]{1,0:T(8,128)}, f32[256,256]{1,0:T(8,128)}) custom-call(f32[512,128]{1,0:T(8,128)S(1)} %bitcast.44, bf16[2,256,128]{2,1,0:T(8,128)(2,1)S(1)} %get-tuple-element.63.refs_1_, f32[2,256,512]{2,1,0:T(8,128)S(1)} %get-tuple-element.64.refs_2_, bf16[2,512,256]{2,1,0:T(8,128)(2,1)} %constant.112.clone.refs_3_, ...), custom_call_target="tpu_custom_call" | custom-call | flops 1800000000 | bytes 6029312 | tf_op jit(solution)/shard_map/pallas_call | solution.py:291
  227.8 22.3 %all_to_all.81 = f32[256,2,128]{2,1,0:T(2,128)S(1)} all-to-all(f32[256,2,128]{2,1,0:T(2,128)} %bitcast.78), channel_id=1, replica_groups=mesh['rows'=64,'cols'=4] {'rows','cols'}, dimensions={0} | all-to-all | bytes 524288 | tf_op jit(solution)/shard_map/all_to_all | solution.py:306
  250.1 2.5 shard_map.164
  252.6 5.8 %all-to-all-start.9 = ((f32[256,1,128]{2,1,0:T(1,128)}), f32[256,1,128]{2,1,0:T(1,128)S(1)}, u32[]{:S(2)}, u32[]{:S(2)}) async-start(f32[256,1,128]{2,1,0:T(1,128)} %bitcast.79), calls=%async_computation.9 | async-start | bytes 262144 | tf_op jit(solution)/shard_map/all_to_all | solution.py:306
  260.2 3.5 shard_map.165
  263.7 7.6 %all-to-all-done.9 = f32[256,1,128]{2,1,0:T(1,128)S(1)} async-done(((f32[256,1,128]{2,1,0:T(1,128)}), f32[256,1,128]{2,1,0:T(1,128)S(1)}, u32[]{:S(2)}, u32[]{:S(2)}) %all-to-all-start.9) | async-done | bytes 131104 | tf_op jit(solution)/shard_map/all_to_all | solution.py:306
  271.4 4.2 shard_map.166
  275.6 6.2 %all-to-all-start.10 = ((f32[256,4,128]{2,1,0:T(4,128)}), f32[256,4,128]{2,1,0:T(4,128)S(1)}, u32[]{:S(2)}, u32[]{:S(2)}) async-start(f32[256,4,128]{2,1,0:T(4,128)} %bitcast.68), calls=%async_computation.10 | async-start | bytes 1048576 | tf_op jit(solution)/shard_map/all_to_all | solution.py:306
  281.9 2.4 shard_map.170
  286.4 3.5 shard_map.171
  292.2 10.9 %all-to-all-done.10 = f32[256,4,128]{2,1,0:T(4,128)S(1)} async-done(((f32[256,4,128]{2,1,0:T(4,128)}), f32[256,4,128]{2,1,0:T(4,128)S(1)}, u32[]{:S(2)}, u32[]{:S(2)}) %all-to-all-start.10) | async-done | bytes 524320 | tf_op jit(solution)/shard_map/all_to_all | solution.py:306
  303.1 2.6 shard_map.168
  305.7 6.0 %all-to-all-start.11 = ((f32[256,1,128]{2,1,0:T(1,128)}), f32[256,1,128]{2,1,0:T(1,128)S(1)}, u32[]{:S(2)}, u32[]{:S(2)}) async-start(f32[256,1,128]{2,1,0:T(1,128)} %bitcast.81), calls=%async_computation.11 | async-start | bytes 262144 | tf_op jit(solution)/shard_map/all_to_all | solution.py:306
  313.4 2.7 shard_map.169.refs_7_
  316.1 8.6 %all-to-all-done.11 = f32[256,1,128]{2,1,0:T(1,128)S(1)} async-done(((f32[256,1,128]{2,1,0:T(1,128)}), f32[256,1,128]{2,1,0:T(1,128)S(1)}, u32[]{:S(2)}, u32[]{:S(2)}) %all-to-all-start.11) | async-done | bytes 131104 | tf_op jit(solution)/shard_map/all_to_all | solution.py:306
  324.7 3.6 shard_map.172
  328.3 6.0 %all-to-all-start.12 = ((f32[256,4,128]{2,1,0:T(4,128)}), f32[256,4,128]{2,1,0:T(4,128)S(1)}, u32[]{:S(2)}, u32[]{:S(2)}) async-start(f32[256,4,128]{2,1,0:T(4,128)} %bitcast.70), calls=%async_computation.12 | async-start | bytes 1048576 | tf_op jit(solution)/shard_map/all_to_all | solution.py:306
  334.3 3.6 shard_map.176
  337.8 2.9 shard_map.173
  340.7 15.0 %all-to-all-done.12 = f32[256,4,128]{2,1,0:T(4,128)S(1)} async-done(((f32[256,4,128]{2,1,0:T(4,128)}), f32[256,4,128]{2,1,0:T(4,128)S(1)}, u32[]{:S(2)}, u32[]{:S(2)}) %all-to-all-start.12) | async-done | bytes 524320 | tf_op jit(solution)/shard_map/all_to_all | solution.py:306
  355.7 3.4 shard_map.174
  359.2 5.7 %all-to-all-start.13 = ((f32[256,1,128]{2,1,0:T(1,128)}), f32[256,1,128]{2,1,0:T(1,128)S(1)}, u32[]{:S(2)}, u32[]{:S(2)}) async-start(f32[256,1,128]{2,1,0:T(1,128)} %bitcast.67), calls=%async_computation.13 | async-start | bytes 262144 | tf_op jit(solution)/shard_map/all_to_all | solution.py:306
  366.6 2.7 shard_map.175.refs_7_
  369.3 8.6 %all-to-all-done.13 = f32[256,1,128]{2,1,0:T(1,128)S(1)} async-done(((f32[256,1,128]{2,1,0:T(1,128)}), f32[256,1,128]{2,1,0:T(1,128)S(1)}, u32[]{:S(2)}, u32[]{:S(2)}) %all-to-all-start.13) | async-done | bytes 131104 | tf_op jit(solution)/shard_map/all_to_all | solution.py:306
  377.9 3.6 shard_map.177
  381.5 6.3 %all-to-all-start.14 = ((f32[256,4,128]{2,1,0:T(4,128)}), f32[256,4,128]{2,1,0:T(4,128)S(1)}, u32[]{:S(2)}, u32[]{:S(2)}) async-start(f32[256,4,128]{2,1,0:T(4,128)} %bitcast.69), calls=%async_computation.14 | async-start | bytes 1048576 | tf_op jit(solution)/shard_map/all_to_all | solution.py:306
  387.9 2.2 shard_map.178.refs_9_
  390.1 4.0 shard_map.179
  394.1 2.6 shard_map.180.refs_8_
  396.7 12.5 %all-to-all-done.14 = f32[256,4,128]{2,1,0:T(4,128)S(1)} async-done(((f32[256,4,128]{2,1,0:T(4,128)}), f32[256,4,128]{2,1,0:T(4,128)S(1)}, u32[]{:S(2)}, u32[]{:S(2)}) %all-to-all-start.14) | async-done | bytes 524320 | tf_op jit(solution)/shard_map/all_to_all | solution.py:306
  409.2 5.6 %shard_map.181 = f32[512,128]{1,0:T(8,128)} custom-call(f32[1024,128]{1,0:T(8,128)S(1)} %bitcast.50, bf16[2,512,256]{2,1,0:T(8,128)(2,1)S(1)} %get-tuple-element.58.refs_1_.refs_4_, f32[2,256,128]{2,1,0:T(8,128)S(1)} %get-tuple-element.59.refs_2_.refs_3_, bf16[2,128,64]{2,1,0:T(8,128)(2,1)S(1)} %get-tuple-element.60.refs_3_, ...), custom_call_target="tpu_custom_call" | custom-call | flops 1200000000 | bytes 2752512 | tf_op jit(solution)/shard_map/pallas_call | solution.py:291
  414.8 5.7 %all-to-all-start.15 = ((f32[256,2,128]{2,1,0:T(2,128)}), f32[256,2,128]{2,1,0:T(2,128)S(1)}, u32[]{:S(2)}, u32[]{:S(2)}) async-start(f32[256,2,128]{2,1,0:T(2,128)} %bitcast.75), calls=%async_computation.15 | async-start | bytes 524288 | tf_op jit(solution)/shard_map/all_to_all | solution.py:306
  420.6 2.8 subtract_subtract_fusion.refs_4_
  423.4 13.1 %all-to-all-done.15 = f32[256,2,128]{2,1,0:T(2,128)S(1)} async-done(((f32[256,2,128]{2,1,0:T(2,128)}), f32[256,2,128]{2,1,0:T(2,128)S(1)}, u32[]{:S(2)}, u32[]{:S(2)}) %all-to-all-start.15) | async-done | bytes 262176 | tf_op jit(solution)/shard_map/all_to_all | solution.py:306
  436.5 3.6 shard_map.182
  (44 shorter events, 14.5 us)
Async XLA Ops:
  4.6 31.5 %all-to-all-start = ((f32[256,2,128]{2,1,0:T(2,128)}), f32[256,2,128]{2,1,0:T(2,128)S(1)}, u32[]{:S(2)}, u32[]{:S(2)}) async-start(f32[256,2,128]{2,1,0:T(2,128)} %bitcast.74), calls=%async_computation | async-start | bytes 524288 | tf_op jit(solution)/shard_map/all_to_all | solution.py:306
  39.7 27.1 %all-to-all-start.1 = ((f32[256,4,128]{2,1,0:T(4,128)}), f32[256,4,128]{2,1,0:T(4,128)S(1)}, u32[]{:S(2)}, u32[]{:S(2)}) async-start(f32[256,4,128]{2,1,0:T(4,128)} %bitcast.72), calls=%async_computation.1 | async-start | bytes 1048576 | tf_op jit(solution)/shard_map/all_to_all | solution.py:306
  70.4 21.8 %all-to-all-start.2 = ((f32[256,2,128]{2,1,0:T(2,128)}), f32[256,2,128]{2,1,0:T(2,128)S(1)}, u32[]{:S(2)}, u32[]{:S(2)}) async-start(f32[256,2,128]{2,1,0:T(2,128)} %bitcast.76), calls=%async_computation.2 | async-start | bytes 524288 | tf_op jit(solution)/shard_map/all_to_all | solution.py:306
  95.6 27.1 %all-to-all-start.3 = ((f32[256,4,128]{2,1,0:T(4,128)}), f32[256,4,128]{2,1,0:T(4,128)S(1)}, u32[]{:S(2)}, u32[]{:S(2)}) async-start(f32[256,4,128]{2,1,0:T(4,128)} %bitcast.73), calls=%async_computation.3 | async-start | bytes 1048576 | tf_op jit(solution)/shard_map/all_to_all | solution.py:306
  148.0 27.8 %all-to-all-start.5 = ((f32[256,4,128]{2,1,0:T(4,128)}), f32[256,4,128]{2,1,0:T(4,128)S(1)}, u32[]{:S(2)}, u32[]{:S(2)}) async-start(f32[256,4,128]{2,1,0:T(4,128)} %bitcast.71), calls=%async_computation.5 | async-start | bytes 1048576 | tf_op jit(solution)/shard_map/all_to_all | solution.py:306
  179.5 18.5 %all-to-all-start.6 = ((f32[256,1,128]{2,1,0:T(1,128)}), f32[256,1,128]{2,1,0:T(1,128)S(1)}, u32[]{:S(2)}, u32[]{:S(2)}) async-start(f32[256,1,128]{2,1,0:T(1,128)} %bitcast.80), calls=%async_computation.6 | async-start | bytes 262144 | tf_op jit(solution)/shard_map/all_to_all | solution.py:306
  200.5 22.0 %all-to-all-start.7 = ((f32[256,2,128]{2,1,0:T(2,128)}), f32[256,2,128]{2,1,0:T(2,128)S(1)}, u32[]{:S(2)}, u32[]{:S(2)}) async-start(f32[256,2,128]{2,1,0:T(2,128)} %bitcast.77), calls=%async_computation.7 | async-start | bytes 524288 | tf_op jit(solution)/shard_map/all_to_all | solution.py:306
  206.5 1.9 copy-start
  206.5 1.9 copy-start.8
  206.5 1.9 copy-start.9
  252.6 5.8 %copy-start.1 = (f32[256,256]{1,0:T(8,128)S(1)}, f32[256,256]{1,0:T(8,128)}, u32[]{:S(2)}) copy-start(f32[256,256]{1,0:T(8,128)} %get-tuple-element.65.refs_6_.refs_10_) | copy-start | bytes 786436
  252.6 18.8 %all-to-all-start.9 = ((f32[256,1,128]{2,1,0:T(1,128)}), f32[256,1,128]{2,1,0:T(1,128)S(1)}, u32[]{:S(2)}, u32[]{:S(2)}) async-start(f32[256,1,128]{2,1,0:T(1,128)} %bitcast.79), calls=%async_computation.9 | async-start | bytes 262144 | tf_op jit(solution)/shard_map/all_to_all | solution.py:306
  275.6 27.5 %all-to-all-start.10 = ((f32[256,4,128]{2,1,0:T(4,128)}), f32[256,4,128]{2,1,0:T(4,128)S(1)}, u32[]{:S(2)}, u32[]{:S(2)}) async-start(f32[256,4,128]{2,1,0:T(4,128)} %bitcast.68), calls=%async_computation.10 | async-start | bytes 1048576 | tf_op jit(solution)/shard_map/all_to_all | solution.py:306
  281.8 2.5 copy-start.7
  281.8 2.5 copy-start.10
  281.8 2.5 copy-start.11
  281.8 2.5 copy-start.12
  281.8 2.5 copy-start.13
  281.9 2.5 copy-start.14
  305.7 6.0 %copy-start.2 = (f32[256,256]{1,0:T(8,128)S(1)}, f32[256,256]{1,0:T(8,128)}, u32[]{:S(2)}) copy-start(f32[256,256]{1,0:T(8,128)} %get-tuple-element.65.refs_6_.refs_10_) | copy-start | bytes 786436
  305.7 18.9 %all-to-all-start.11 = ((f32[256,1,128]{2,1,0:T(1,128)}), f32[256,1,128]{2,1,0:T(1,128)S(1)}, u32[]{:S(2)}, u32[]{:S(2)}) async-start(f32[256,1,128]{2,1,0:T(1,128)} %bitcast.81), calls=%async_computation.11 | async-start | bytes 262144 | tf_op jit(solution)/shard_map/all_to_all | solution.py:306
  328.3 27.5 %all-to-all-start.12 = ((f32[256,4,128]{2,1,0:T(4,128)}), f32[256,4,128]{2,1,0:T(4,128)S(1)}, u32[]{:S(2)}, u32[]{:S(2)}) async-start(f32[256,4,128]{2,1,0:T(4,128)} %bitcast.70), calls=%async_computation.12 | async-start | bytes 1048576 | tf_op jit(solution)/shard_map/all_to_all | solution.py:306
  359.2 5.7 %copy-start.3 = (f32[256,256]{1,0:T(8,128)S(1)}, f32[256,256]{1,0:T(8,128)}, u32[]{:S(2)}) copy-start(f32[256,256]{1,0:T(8,128)} %get-tuple-element.65.refs_6_.refs_10_) | copy-start | bytes 786436
  359.2 18.7 %all-to-all-start.13 = ((f32[256,1,128]{2,1,0:T(1,128)}), f32[256,1,128]{2,1,0:T(1,128)S(1)}, u32[]{:S(2)}, u32[]{:S(2)}) async-start(f32[256,1,128]{2,1,0:T(1,128)} %bitcast.67), calls=%async_computation.13 | async-start | bytes 262144 | tf_op jit(solution)/shard_map/all_to_all | solution.py:306
  381.5 27.7 %all-to-all-start.14 = ((f32[256,4,128]{2,1,0:T(4,128)}), f32[256,4,128]{2,1,0:T(4,128)S(1)}, u32[]{:S(2)}, u32[]{:S(2)}) async-start(f32[256,4,128]{2,1,0:T(4,128)} %bitcast.69), calls=%async_computation.14 | async-start | bytes 1048576 | tf_op jit(solution)/shard_map/all_to_all | solution.py:306
  409.2 11.4 %copy-start.6 = (f32[256,256]{1,0:T(8,128)S(1)}, f32[256,256]{1,0:T(8,128)}, u32[]{:S(2)}) copy-start(f32[256,256]{1,0:T(8,128)} %get-tuple-element.103) | copy-start | bytes 786436
  414.8 5.8 %copy-start.4 = (f32[256,256]{1,0:T(8,128)S(1)}, f32[256,256]{1,0:T(8,128)}, u32[]{:S(2)}) copy-start(f32[256,256]{1,0:T(8,128)} %get-tuple-element.65.refs_6_.refs_10_) | copy-start | bytes 786436
  414.8 5.8 %copy-start.5 = (f32[256,256]{1,0:T(8,128)S(1)}, f32[256,256]{1,0:T(8,128)}, u32[]{:S(2)}) copy-start(f32[256,256]{1,0:T(8,128)} %get-tuple-element.95) | copy-start | bytes 786436
  414.8 21.7 %all-to-all-start.15 = ((f32[256,2,128]{2,1,0:T(2,128)}), f32[256,2,128]{2,1,0:T(2,128)S(1)}, u32[]{:S(2)}, u32[]{:S(2)}) async-start(f32[256,2,128]{2,1,0:T(2,128)} %bitcast.75), calls=%async_computation.15 | async-start | bytes 524288 | tf_op jit(solution)/shard_map/all_to_all | solution.py:306
